TPU v7x, 128 devices: a whole 4x4x4 slice. The times are simulated.
128 devices in a mesh: dp: 8 (over z, core), own: 16 (over x, y).
Axes of the slice: x: 4, y: 4, z: 4, core: 2. Of those that a mesh axis runs over, the one named last changes fastest.
Arguments:
- queries: float32 [262144, 128], P(('dp', 'own')), may hold values from -24 to 24
- positives: float32 [262144, 128], P(('dp', 'own')), may hold values from -6 to 6
- neg_ids: int32 [2048, 512], P(('dp', 'own')), may hold values from 0 to 131071, as said below
- table: float32 [131072, 128], P('own'), may hold values from -6 to 6
- accum: float32 [131072, 128], P('own'), may hold values from 1e-07 to 1e-05
Outputs:
- new_table: float32 [131072, 128], P('own')
- query_grad: float32 [262144, 128], P(('dp', 'own'))
Inputs may be any that keep to these rules, and one draw needn't show every extreme that they name: Row r of neg_ids holds rows of owner r % 16 only: ids from (r % 16) * 8192 to (r % 16 + 1) * 8192 - 1. Every row holds exactly 256 distinct ids, each appearing one or more times.
All inputs are finite; a program needn't handle non-finite values.
Results may differ from a plain program's by a relative error of at most 0.0003.
Values sent between devices are 32-bit elements; how exact they have to be, the bound alone decides.
A program may use at most 128 MiB of HBM per device.

v0:
```python
import jax
import jax.numpy as jnp
from jax import lax
from jax.sharding import PartitionSpec as P


def adagrad(table_rows, accum_rows, grad):
    new_accum = accum_rows + grad * grad
    return table_rows - 0.5 * grad / (jnp.sqrt(new_accum) + 1e-08)


def local(queries, positives, neg_ids, table, accum):
    owners = lax.axis_size("own")
    rows_dev = table.shape[0]
    width = table.shape[1]
    first_row = lax.axis_index("own") * rows_dev
    received = lax.all_to_all(neg_ids, "own", split_axis=0, concat_axis=0, tiled=True)
    local_ids = received - first_row
    returned = lax.all_to_all(
        jnp.take(table, local_ids.reshape(-1), axis=0).reshape(local_ids.shape + (width,)),
        "own",
        split_axis=0,
        concat_axis=0,
        tiled=True,
    )
    neg_rows = returned
    weights = jnp.ones((neg_ids.shape[0] * neg_ids.shape[1],), jnp.float32)
    neg_rows = neg_rows.reshape(-1, width)
    negatives = neg_rows.shape[0]
    count = queries.shape[0]
    block = min(512, count)
    query_blocks = queries.reshape(count // block, block, width)
    positive_blocks = positives.reshape(count // block, block, width)

    def score_block(total_grad, items):
        query_rows, positive_rows = items
        pos_score = jnp.sum(query_rows * positive_rows, axis=1)
        neg_scores = jnp.dot(query_rows, neg_rows.T, precision=lax.Precision.HIGHEST)
        top = jnp.maximum(pos_score, jnp.max(neg_scores, axis=1))
        pos_exp = jnp.exp(pos_score - top)
        neg_exp = jnp.exp(neg_scores - top[:, None]) * weights[None, :]
        total = pos_exp + jnp.sum(neg_exp, axis=1)
        pos_dz = pos_exp / total - 1.0
        neg_dz = neg_exp / total[:, None]
        query_grad = pos_dz[:, None] * positive_rows + jnp.dot(
            neg_dz, neg_rows, precision=lax.Precision.HIGHEST
        )
        neg_grad = jnp.dot(neg_dz.T, query_rows, precision=lax.Precision.HIGHEST)
        return (total_grad + neg_grad, query_grad)

    neg_grad, query_grad = lax.scan(
        score_block, jnp.zeros((negatives, width), jnp.float32), (query_blocks, positive_blocks)
    )
    query_grad = query_grad.reshape(count, width)
    arrived = lax.all_to_all(
        neg_grad.reshape(owners, -1, width), "own", split_axis=0, concat_axis=0, tiled=True
    )
    flat_grads = arrived.reshape(-1, width)
    local_ids = (received - first_row).reshape(-1)
    dense = jax.ops.segment_sum(flat_grads, local_ids, num_segments=rows_dev)
    summed = lax.psum(dense, "dp")
    new_table = adagrad(table, accum, summed)
    return (new_table, query_grad)


def solution(mesh):
    return jax.shard_map(
        local,
        mesh=mesh,
        in_specs=(
            P(("dp", "own"), None),
            P(("dp", "own"), None),
            P(("dp", "own"), None),
            P("own", None),
            P("own", None),
        ),
        out_specs=(P("own", None), P(("dp", "own"), None)),
        check_vma=False,
    )
```

profile of v0, /device:TPU:1, one launch (start us, length us, event | category | flops | bytes accessed | tf_op | source)
XLA Modules:
  0.0 626.8 jit_solution(7086878567699321178)
XLA Ops:
  8.6 7.6 %all-to-all-start = ((s32[16,1,512]{2,1,0:T(1,128)}), s32[16,1,512]{2,1,0:T(1,128)S(1)}, u32[]{:S(2)}, u32[]{:S(2)}) async-start(s32[16,1,512]{2,1,0:T(1,128)} %all_to_all.12), calls=%async_computation | async-start | bytes 65536 | tf_op jit(solution)/shard_map/all_to_all | solution.py:17
  23.3 30.1 %gather_fusion = f32[8192,128]{1,0:T(8,128)} fusion(f32[8192,128]{1,0:T(8,128)} %param.10, s32[8192]{0:T(1024)S(1)} %broadcast_clamp_fusion), kind=kCustom, calls=%fused_computation | custom fusion | bytes 8421376 | tf_op jit(solution)/shard_map/jit(_take)/gather | solution.py:20
  63.4 51.6 %all-to-all-done.1 = f32[16,512,128]{2,1,0:T(8,128)} async-done(((f32[16,512,128]{2,1,0:T(8,128)}), f32[16,512,128]{2,1,0:T(8,128)}, u32[]{:S(2)}, u32[]{:S(2)}) %all-to-all-start.1) | async-done | bytes 4194336 | tf_op jit(solution)/shard_map/all_to_all | solution.py:19
  115.0 323.3 %while.15 = (s32[]{:T(128)}, f32[8192,128]{1,0:T(8,128)}, f32[4,512,128]{2,1,0:T(8,128)}, f32[4,512,128]{2,1,0:T(8,128)S(1)}, f32[8192,128]{1,0:T(8,128)}, /*index=5*/f32[4,512,128]{2,1,0:T(8,128)S(1)}, s32[]{:T(128)}, s32[]{:T(128)}) while((s32[]{:T(128)}, f32[8192,128]{1,0:T(8,128)}, f32[4,512,128]{2,1,0:T(8,128)}, ...), condition=%wide.region_4.5_spmd.clone, body=%wide.region_0.4_spmd.clone.sunk | while | flops 19359072256 | bytes 85494376 | solution.py:51
  115.0 17.3 %fusion.34 = (f32[512]{0:T(512)S(1)}, f32[512,8192]{1,0:T(8,128)}) fusion(f32[8192,128]{1,0:T(8,128)} %get-tuple-element.184, f32[4,512,128]{2,1,0:T(8,128)S(1)} %get-tuple-element.183, s32[]{:T(128)} %get-tuple-element.172), kind=kOutput, calls=%fused_computation.31.clone.1 | convolution fusion | flops 6446644736 | bytes 21235716 | tf_op jit(solution)/shard_map/while/body/eval_jaxpr/dot_general | solution.py:38
  132.5 8.1 %fusion.36 = f32[512]{0:T(512)S(1)} fusion(f32[512,8192]{1,0:T(8,128)} %get-tuple-element.160, f32[512]{0:T(512)S(1)} %max.24), kind=kLoop, calls=%fused_computation.4.clone.1 | loop fusion | flops 8388096 | bytes 16781312 | tf_op jit(solution)/shard_map/while/body/eval_jaxpr/reduce_sum | solution.py:42
  140.6 23.1 %fusion.37 = f32[4,512,128]{2,1,0:T(8,128)} fusion(f32[4,512,128]{2,1,0:T(8,128)} %get-tuple-element.174, s32[]{:T(128)} %get-tuple-element.172, f32[8192,128]{1,0:T(8,128)} %get-tuple-element.184, f32[4,512,128]{2,1,0:T(8,128)S(1)} %get-tuple-element.185, f32[512]{0:T(512)S(1)} %get-tuple-element.163, f32[512,8192]{1,0:T(8,128)} %get-tuple-element.160, ...), kind=kOutput, calls=%fused_computation.8.clone.1 | convolution fusion | flops 6450970624 | bytes 21502464 | tf_op jit(solution)/shard_map/while/body/eval_jaxpr/dot_general | solution.py:45
  163.7 31.8 %convolution_add_fusion.3 = f32[8192,128]{1,0:T(8,128)} fusion(f32[8192,128]{1,0:T(8,128)} %get-tuple-element.173, pred[]{:T(512)S(6)} %compare.3, f32[4,512,128]{2,1,0:T(8,128)S(1)} %get-tuple-element.183, s32[]{:T(128)} %get-tuple-element.172, f32[512,8192]{1,0:T(8,128)} %get-tuple-element.160, f32[512]{0:T(512)S(1)} %get-tuple-element.162, ...), kind=kOutput, calls=%fused_computation.5.clone.1 | convolution fusion | flops 6452936704 | bytes 25432068 | tf_op jit(solution)/shard_map/while/body/eval_jaxpr/dot_general | solution.py:48
  195.5 17.3 %fusion.34 = (f32[512]{0:T(512)S(1)}, f32[512,8192]{1,0:T(8,128)}) fusion(f32[8192,128]{1,0:T(8,128)} %get-tuple-element.184, f32[4,512,128]{2,1,0:T(8,128)S(1)} %get-tuple-element.183, s32[]{:T(128)} %get-tuple-element.172), kind=kOutput, calls=%fused_computation.31.clone.1 | convolution fusion | flops 6446644736 | bytes 21235716 | tf_op jit(solution)/shard_map/while/body/eval_jaxpr/dot_general | solution.py:38
  213.0 8.1 %fusion.36 = f32[512]{0:T(512)S(1)} fusion(f32[512,8192]{1,0:T(8,128)} %get-tuple-element.160, f32[512]{0:T(512)S(1)} %max.24), kind=kLoop, calls=%fused_computation.4.clone.1 | loop fusion | flops 8388096 | bytes 16781312 | tf_op jit(solution)/shard_map/while/body/eval_jaxpr/reduce_sum | solution.py:42
  221.1 23.1 %fusion.37 = f32[4,512,128]{2,1,0:T(8,128)} fusion(f32[4,512,128]{2,1,0:T(8,128)} %get-tuple-element.174, s32[]{:T(128)} %get-tuple-element.172, f32[8192,128]{1,0:T(8,128)} %get-tuple-element.184, f32[4,512,128]{2,1,0:T(8,128)S(1)} %get-tuple-element.185, f32[512]{0:T(512)S(1)} %get-tuple-element.163, f32[512,8192]{1,0:T(8,128)} %get-tuple-element.160, ...), kind=kOutput, calls=%fused_computation.8.clone.1 | convolution fusion | flops 6450970624 | bytes 21502464 | tf_op jit(solution)/shard_map/while/body/eval_jaxpr/dot_general | solution.py:45
  244.2 32.3 %convolution_add_fusion.3 = f32[8192,128]{1,0:T(8,128)} fusion(f32[8192,128]{1,0:T(8,128)} %get-tuple-element.173, pred[]{:T(512)S(6)} %compare.3, f32[4,512,128]{2,1,0:T(8,128)S(1)} %get-tuple-element.183, s32[]{:T(128)} %get-tuple-element.172, f32[512,8192]{1,0:T(8,128)} %get-tuple-element.160, f32[512]{0:T(512)S(1)} %get-tuple-element.162, ...), kind=kOutput, calls=%fused_computation.5.clone.1 | convolution fusion | flops 6452936704 | bytes 25432068 | tf_op jit(solution)/shard_map/while/body/eval_jaxpr/dot_general | solution.py:48
  276.4 17.3 %fusion.34 = (f32[512]{0:T(512)S(1)}, f32[512,8192]{1,0:T(8,128)}) fusion(f32[8192,128]{1,0:T(8,128)} %get-tuple-element.184, f32[4,512,128]{2,1,0:T(8,128)S(1)} %get-tuple-element.183, s32[]{:T(128)} %get-tuple-element.172), kind=kOutput, calls=%fused_computation.31.clone.1 | convolution fusion | flops 6446644736 | bytes 21235716 | tf_op jit(solution)/shard_map/while/body/eval_jaxpr/dot_general | solution.py:38
  293.9 8.1 %fusion.36 = f32[512]{0:T(512)S(1)} fusion(f32[512,8192]{1,0:T(8,128)} %get-tuple-element.160, f32[512]{0:T(512)S(1)} %max.24), kind=kLoop, calls=%fused_computation.4.clone.1 | loop fusion | flops 8388096 | bytes 16781312 | tf_op jit(solution)/shard_map/while/body/eval_jaxpr/reduce_sum | solution.py:42
  302.0 23.1 %fusion.37 = f32[4,512,128]{2,1,0:T(8,128)} fusion(f32[4,512,128]{2,1,0:T(8,128)} %get-tuple-element.174, s32[]{:T(128)} %get-tuple-element.172, f32[8192,128]{1,0:T(8,128)} %get-tuple-element.184, f32[4,512,128]{2,1,0:T(8,128)S(1)} %get-tuple-element.185, f32[512]{0:T(512)S(1)} %get-tuple-element.163, f32[512,8192]{1,0:T(8,128)} %get-tuple-element.160, ...), kind=kOutput, calls=%fused_computation.8.clone.1 | convolution fusion | flops 6450970624 | bytes 21502464 | tf_op jit(solution)/shard_map/while/body/eval_jaxpr/dot_general | solution.py:45
  325.1 32.3 %convolution_add_fusion.3 = f32[8192,128]{1,0:T(8,128)} fusion(f32[8192,128]{1,0:T(8,128)} %get-tuple-element.173, pred[]{:T(512)S(6)} %compare.3, f32[4,512,128]{2,1,0:T(8,128)S(1)} %get-tuple-element.183, s32[]{:T(128)} %get-tuple-element.172, f32[512,8192]{1,0:T(8,128)} %get-tuple-element.160, f32[512]{0:T(512)S(1)} %get-tuple-element.162, ...), kind=kOutput, calls=%fused_computation.5.clone.1 | convolution fusion | flops 6452936704 | bytes 25432068 | tf_op jit(solution)/shard_map/while/body/eval_jaxpr/dot_general | solution.py:48
  357.3 17.3 %fusion.34 = (f32[512]{0:T(512)S(1)}, f32[512,8192]{1,0:T(8,128)}) fusion(f32[8192,128]{1,0:T(8,128)} %get-tuple-element.184, f32[4,512,128]{2,1,0:T(8,128)S(1)} %get-tuple-element.183, s32[]{:T(128)} %get-tuple-element.172), kind=kOutput, calls=%fused_computation.31.clone.1 | convolution fusion | flops 6446644736 | bytes 21235716 | tf_op jit(solution)/shard_map/while/body/eval_jaxpr/dot_general | solution.py:38
  374.8 8.1 %fusion.36 = f32[512]{0:T(512)S(1)} fusion(f32[512,8192]{1,0:T(8,128)} %get-tuple-element.160, f32[512]{0:T(512)S(1)} %max.24), kind=kLoop, calls=%fused_computation.4.clone.1 | loop fusion | flops 8388096 | bytes 16781312 | tf_op jit(solution)/shard_map/while/body/eval_jaxpr/reduce_sum | solution.py:42
  382.9 23.1 %fusion.37 = f32[4,512,128]{2,1,0:T(8,128)} fusion(f32[4,512,128]{2,1,0:T(8,128)} %get-tuple-element.174, s32[]{:T(128)} %get-tuple-element.172, f32[8192,128]{1,0:T(8,128)} %get-tuple-element.184, f32[4,512,128]{2,1,0:T(8,128)S(1)} %get-tuple-element.185, f32[512]{0:T(512)S(1)} %get-tuple-element.163, f32[512,8192]{1,0:T(8,128)} %get-tuple-element.160, ...), kind=kOutput, calls=%fused_computation.8.clone.1 | convolution fusion | flops 6450970624 | bytes 21502464 | tf_op jit(solution)/shard_map/while/body/eval_jaxpr/dot_general | solution.py:45
  406.0 32.3 %convolution_add_fusion.3 = f32[8192,128]{1,0:T(8,128)} fusion(f32[8192,128]{1,0:T(8,128)} %get-tuple-element.173, pred[]{:T(512)S(6)} %compare.3, f32[4,512,128]{2,1,0:T(8,128)S(1)} %get-tuple-element.183, s32[]{:T(128)} %get-tuple-element.172, f32[512,8192]{1,0:T(8,128)} %get-tuple-element.160, f32[512]{0:T(512)S(1)} %get-tuple-element.162, ...), kind=kOutput, calls=%fused_computation.5.clone.1 | convolution fusion | flops 6452936704 | bytes 25432068 | tf_op jit(solution)/shard_map/while/body/eval_jaxpr/dot_general | solution.py:48
  438.3 50.9 %all_to_all.19 = f32[16,512,128]{2,1,0:T(8,128)} all-to-all(f32[16,512,128]{2,1,0:T(8,128)} %bitcast.55), channel_id=1, replica_groups=mesh['dp'=8,'own'=16] {'own'}, dimensions={0} | all-to-all | bytes 8388608 | tf_op jit(solution)/shard_map/all_to_all | solution.py:55
  489.2 46.5 %scatter_custom_fusion = f32[8192,128]{1,0:T(8,128)} fusion(s32[8192]{0:T(1024)} %bitcast.60, f32[8192,128]{1,0:T(8,128)} %bitcast.56, f32[]{:T(128)} %constant.55.clone.1), kind=kCustom, calls=%fused_computation.24 | custom fusion | flops 1048576 | bytes 4194816 | tf_op jit(solution)/shard_map/scatter-add | solution.py:60
  535.7 75.7 %all-reduce.2.cloned.1.call-done = f32[8192,128]{1,0:T(8,128)} async-done(((f32[8192,128]{1,0:T(8,128)}), f32[8192,128]{1,0:T(8,128)}) %all-reduce.2.cloned.1.call-update) | async-done | bytes 4194320 | tf_op jit(solution)/shard_map/psum | solution.py:61
  611.4 8.6 %divide_subtract_fusion = f32[8192,128]{1,0:T(8,128)} fusion(f32[8192,128]{1,0:T(8,128)} %param.10, f32[8192,128]{1,0:T(8,128)} %param.11, f32[8192,128]{1,0:T(8,128)} %all-reduce.2.cloned.1.call-done), kind=kLoop, calls=%fused_computation.22 | loop fusion | flops 6291456 | bytes 16777216 | tf_op jit(solution)/shard_map/sub | solution.py:9
  (30 shorter events, 19.1 us)
Async XLA Ops:
  8.6 14.1 %all-to-all-start = ((s32[16,1,512]{2,1,0:T(1,128)}), s32[16,1,512]{2,1,0:T(1,128)S(1)}, u32[]{:S(2)}, u32[]{:S(2)}) async-start(s32[16,1,512]{2,1,0:T(1,128)} %all_to_all.12), calls=%async_computation | async-start | bytes 65536 | tf_op jit(solution)/shard_map/all_to_all | solution.py:17
  22.6 0.6 copy-start.2
  58.7 56.3 %copy-start = (f32[2048,128]{1,0:T(8,128)S(1)}, f32[2048,128]{1,0:T(8,128)}, u32[]{:S(2)}) copy-start(f32[2048,128]{1,0:T(8,128)} %param.7) | copy-start | bytes 3145732
  58.7 56.3 %copy-start.1 = (f32[2048,128]{1,0:T(8,128)S(1)}, f32[2048,128]{1,0:T(8,128)}, u32[]{:S(2)}) copy-start(f32[2048,128]{1,0:T(8,128)} %param.8) | copy-start | bytes 3145732
  58.7 56.3 %all-to-all-start.1 = ((f32[16,512,128]{2,1,0:T(8,128)}), f32[16,512,128]{2,1,0:T(8,128)}, u32[]{:S(2)}, u32[]{:S(2)}) async-start(f32[16,512,128]{2,1,0:T(8,128)} %broadcast_select_fusion), calls=%async_computation.1 | async-start | bytes 8388608 | tf_op jit(solution)/shard_map/all_to_all | solution.py:19
  63.4 548.0 %all-reduce.2.cloned.1.call-start = ((), (), s32[]{:S(2)}) async-start(), calls=%async_computation.3 | async-start | bytes 8388608 | tf_op jit(solution)/shard_map/psum | solution.py:61
Sparse Core Ops, SparseCore 0:
  535.8 75.4 all-reduce.1
where the time goes:
time: 629 us; the launch traced here: 627 us
  matrix products  290 us (46%)
  waiting for transfers between devices  134 us (21%)
  other arithmetic  93.5 us (15%)
  blocking collectives  50.9 us (8%)
  local copies, waits for them, and re-layouts  32.1 us (5%)
  between operations  14.1 us (2%)
  starting transfers between devices  12.3 us (2%)
    dot_general x4, matrix products, score_block(): neg_grad = jnp.dot(neg_dz.T, query_rows, precision=lax.Precision.HIGHEST)  129 us
    dot_general x4, matrix products, score_block(): jnp.dot(neg_dz, neg_rows, precision=lax.Precision.HIGHEST)  92.3 us
    psum x1, waiting for transfers between devices, local(): summed = lax.psum(dense, 'dp')  75.7 us
    dot_general x4, matrix products, score_block(): jnp.dot(query_rows, neg_rows.T, precision=lax.Precision.HIGHEST)  69.3 us
    all_to_all x1, waiting for transfers between devices, local(): lax.all_to_all(jnp.take(table, local_ids.reshape(-1), axis=0).reshape(loc...  51.6 us
    all_to_all x1, blocking collectives, local(): lax.all_to_all(neg_grad.reshape(owners, -1, width), 'own', split_axis=0,...  50.9 us
    scatter-add x1, other arithmetic, local(): dense = jax.ops.segment_sum(flat_grads, local_ids, num_segments=rows_dev)  46.5 us
    reduce_sum x4, other arithmetic, score_block(): total = pos_exp + jnp.sum(neg_exp, axis=1)  32.4 us
  transfers between devices with their start and end apart: 3, of which 3 were waited for; matrix products, arithmetic and copies ran while one was open for 0% of the time, Pallas kernels for 0%

commit v1 on v0

v1 whole, which is shorter than its diff:
```python
import functools
import jax
import jax.numpy as jnp
from jax import lax
from jax.experimental import pallas as pl
from jax.experimental.pallas import tpu as pltpu
from jax.sharding import PartitionSpec as P

F32, BF16, I32 = jnp.float32, jnp.bfloat16, jnp.int32
LOG2E = 1.4426950408889634
MIB = 1024 * 1024


def split(x):
    hi = x.astype(BF16)
    return hi, (x - hi.astype(F32)).astype(BF16)


def dot(a, b):
    return lax.dot_general(a, b, (((1,), (0,)), ((), ())), preferred_element_type=F32)


def dot_t(a, b):
    return lax.dot_general(a, b, (((1,), (1,)), ((), ())), preferred_element_type=F32)


def dedup_kernel(rows_dev, ids_ref, out_ref, cnt_ref):
    owners, per = ids_ref.shape
    few = 256
    base = lax.broadcasted_iota(I32, (owners, per), 0) * rows_dev
    local = (ids_ref[...] - base).astype(F32)
    cols = jnp.transpose(jnp.concatenate([local, jnp.zeros((128 - owners, per), F32)], axis=0))
    lane = lax.broadcasted_iota(I32, (128, per), 1)
    sub = lax.broadcasted_iota(I32, (128, per), 0)
    firsts, counts = [], []
    for r in range(owners):
        row = local[r : r + 1, :]
        count = jnp.zeros((1, per), F32)
        before = jnp.zeros((1, per), F32)
        for b in range(per // 128):
            col = cols[b * 128 : (b + 1) * 128, r : r + 1]
            eq = jnp.where(col == row, 1.0, 0.0)
            count = count + jnp.sum(eq, axis=0, keepdims=True)
            before = before + jnp.sum(jnp.where(sub + b * 128 < lane, eq, 0.0), axis=0, keepdims=True)
        firsts.append(before < 0.5)
        counts.append(count)
    first = jnp.concatenate([jnp.where(f, 1.0, 0.0) for f in firsts], axis=0)
    count = jnp.concatenate(counts, axis=0)
    tri = jnp.where(
        lax.broadcasted_iota(I32, (per, per), 0) < lax.broadcasted_iota(I32, (per, per), 1), 1.0, 0.0
    ).astype(BF16)
    place = dot(first.astype(BF16), tri)
    place = jnp.where(first > 0.5, place, -1.0).astype(I32)
    li = local.astype(I32)
    ci = count.astype(I32)
    parts = [(li >> 7).astype(F32), (li & 127).astype(F32), (ci >> 4).astype(F32), (ci & 15).astype(F32)]
    slot = lax.broadcasted_iota(I32, (few, per), 0)
    for r in range(owners):
        hot = jnp.where(slot == place[r : r + 1, :], 1.0, 0.0).astype(BF16)
        vals = jnp.concatenate([p[r : r + 1, :] for p in parts] + [jnp.zeros((12, per), F32)], axis=0)
        got = dot_t(vals.astype(BF16), hot)
        ids = got[0:1, :] * 128.0 + got[1:2, :]
        cnt = got[2:3, :] * 16.0 + got[3:4, :]
        both = jnp.concatenate([ids[:, :128], ids[:, 128:], jnp.zeros((6, 128), F32)], axis=0)
        out_ref[r] = both.astype(I32)
        cnt_ref[r] = jnp.broadcast_to(cnt, (8, few))


def dedup(ids, rows_dev):
    owners, per = ids.shape
    return pl.pallas_call(
        functools.partial(dedup_kernel, rows_dev),
        out_shape=(
            jax.ShapeDtypeStruct((owners, 8, 128), I32),
            jax.ShapeDtypeStruct((owners, 8, 256), F32),
        ),
        in_specs=[pl.BlockSpec(memory_space=pltpu.VMEM)],
        out_specs=(pl.BlockSpec(memory_space=pltpu.VMEM),) * 2,
        compiler_params=pltpu.CompilerParams(vmem_limit_bytes=16 * MIB),
        name="dedup",
    )(ids)


def gather_kernel(ids_ref, table_ref, out_ref):
    few = out_ref.shape[1]

    def block(s, c):
        def group(g, c):
            for i in range(16):
                j = g * 16 + i
                out_ref[s, pl.ds(j, 1), :] = table_ref[pl.ds(ids_ref[s, j >> 7, j & 127], 1), :]
            return c
        return lax.fori_loop(0, few // 16, group, c)

    lax.fori_loop(0, out_ref.shape[0], block, 0)


def gather(ids, table):
    return pl.pallas_call(
        gather_kernel,
        out_shape=jax.ShapeDtypeStruct((ids.shape[0], 256, 128), F32),
        in_specs=[pl.BlockSpec(memory_space=pltpu.SMEM), pl.BlockSpec(memory_space=pltpu.VMEM)],
        out_specs=pl.BlockSpec(memory_space=pltpu.VMEM),
        compiler_params=pltpu.CompilerParams(vmem_limit_bytes=32 * MIB),
        name="gather",
    )(ids, table)


def scatter_kernel(ids_ref, grad_ref, out_ref):
    few = grad_ref.shape[1]
    out_ref[...] = jnp.zeros_like(out_ref)

    def block(s, c):
        def group(g, c):
            at, vals = [], []
            for i in range(16):
                j = g * 16 + i
                at.append(ids_ref[s, j >> 7, j & 127])
                vals.append(out_ref[pl.ds(at[i], 1), :] + grad_ref[s, pl.ds(j, 1), :])
            for i in range(16):
                out_ref[pl.ds(at[i], 1), :] = vals[i]
            return c
        return lax.fori_loop(0, few // 16, group, c)

    lax.fori_loop(0, grad_ref.shape[0], block, 0)


def scatter(ids, grads, rows_dev):
    return pl.pallas_call(
        scatter_kernel,
        out_shape=jax.ShapeDtypeStruct((rows_dev, 128), F32),
        in_specs=[pl.BlockSpec(memory_space=pltpu.SMEM), pl.BlockSpec(memory_space=pltpu.VMEM)],
        out_specs=pl.BlockSpec(memory_space=pltpu.VMEM),
        compiler_params=pltpu.CompilerParams(vmem_limit_bytes=32 * MIB),
        name="scatter",
    )(ids, grads)


def prepare(q_ref, p_ref, qtf, ptf, qt2, m, total, qacc):
    count = q_ref.shape[0]
    for t in range(count // 128):
        tile = pl.ds(t * 128, 128)
        qt = jnp.transpose(q_ref[tile, :])
        pt = jnp.transpose(p_ref[tile, :])
        qtf[:, tile] = qt
        ptf[:, tile] = pt
        hi, lo = split(qt * LOG2E)
        qt2[0:128, tile] = hi
        qt2[128:256, tile] = lo
        m[0:1, tile] = jnp.sum(qt * pt, axis=0, keepdims=True) * LOG2E
    total[...] = jnp.ones_like(total)
    qacc[...] = ptf[...]


def phase_a(n, w, s, qt2, m, ms, total, qacc, eh, el, tq):
    hi, lo = split(n)
    nt = jnp.transpose(n) * w
    nth, ntl = split(nt)
    wh, wl = split(w)
    sub = lax.broadcasted_iota(I32, (16, 256), 0)
    wrows = jnp.where(sub == 0, wh.astype(F32), jnp.where(sub == 1, wl.astype(F32), 0.0)).astype(BF16)
    left1 = jnp.concatenate([nth, wrows, ntl], axis=0)
    left2 = left1[0:144]
    n1 = jnp.concatenate([hi, hi], axis=1)
    n2 = jnp.concatenate([lo, lo], axis=1)
    count = qt2.shape[1]
    for t in range(count // tq):
        tile = pl.ds(t * tq, tq)
        right = qt2[:, tile]
        score = dot(n1, right) + dot(n2, right)
        old = m[0:1, tile]
        new = jnp.maximum(old, jnp.max(score, axis=0, keepdims=True))
        alpha = jnp.exp2(old - new)
        m[0:1, tile] = new
        ms[s, 0:1, tile] = new
        e = jnp.exp2(score - new)
        h, l = split(e)
        eh[s, :, tile] = h
        el[s, :, tile] = l
        a1 = dot(left1, h)
        a2 = dot(left2, l)
        total[0:1, tile] = (
            total[0:1, tile] * alpha + (a1[128:129] + a1[129:130]) + (a2[128:129] + a2[129:130])
        )
        qacc[:, tile] = qacc[:, tile] * alpha + (a1[0:128] + (a1[144:272] + a2[0:128]))


def finish(qg_ref, ptf, m, total, qacc):
    count = qacc.shape[1]
    for t in range(count // 128):
        tile = pl.ds(t * 128, 128)
        g = qacc[:, tile] * (1.0 / total[0:1, tile]) - ptf[:, tile]
        qg_ref[tile, :] = jnp.transpose(g)


def phase_b(w, s, qtf, m, ms, total, eh, el):
    c = jnp.exp2(ms[s, 0:1, :] - m[0:1, :]) * (1.0 / total[0:1, :])
    qh, ql = split(qtf[...] * c)
    g1 = dot_t(eh[s], jnp.concatenate([qh, ql], axis=0))
    g2 = dot_t(el[s], qh)
    wc = jnp.transpose(jnp.broadcast_to(w, (128, 256)))
    return wc * (g1[:, 0:128] + (g1[:, 128:256] + g2))


def compute_kernel(tq, q_ref, p_ref, n_ref, w_ref, qg_ref, g_ref, qtf, ptf, qt2, m, ms, total, qacc, eh, el):
    prepare(q_ref, p_ref, qtf, ptf, qt2, m, total, qacc)

    def a(s, c):
        phase_a(n_ref[s], w_ref[s, 0:1, :], s, qt2, m, ms, total, qacc, eh, el, tq)
        return c

    lax.fori_loop(0, n_ref.shape[0], a, 0)
    finish(qg_ref, ptf, m, total, qacc)

    def b(s, c):
        g_ref[s] = phase_b(w_ref[s, 0:1, :], s, qtf, m, ms, total, eh, el)
        return c

    lax.fori_loop(0, n_ref.shape[0], b, 0)


def compute_scratch(count, owners):
    return [
        pltpu.VMEM((128, count), F32),
        pltpu.VMEM((128, count), F32),
        pltpu.VMEM((256, count), BF16),
        pltpu.VMEM((8, count), F32),
        pltpu.VMEM((owners, 8, count), F32),
        pltpu.VMEM((8, count), F32),
        pltpu.VMEM((128, count), F32),
        pltpu.VMEM((owners, 256, count), BF16),
        pltpu.VMEM((owners, 256, count), BF16),
    ]


def compute(q, p, n, w, tq=512):
    count, owners = q.shape[0], n.shape[0]
    vm = pl.BlockSpec(memory_space=pltpu.VMEM)
    return pl.pallas_call(
        functools.partial(compute_kernel, tq),
        out_shape=(jax.ShapeDtypeStruct((count, 128), F32), jax.ShapeDtypeStruct((owners, 256, 128), F32)),
        in_specs=[vm] * 4,
        out_specs=(vm, vm),
        scratch_shapes=compute_scratch(count, owners),
        compiler_params=pltpu.CompilerParams(vmem_limit_bytes=60 * MIB),
        name="compute",
    )(q, p, n, w)


def adagrad(table_rows, accum_rows, grad):
    new_accum = accum_rows + grad * grad
    return table_rows - 0.5 * grad / (jnp.sqrt(new_accum) + 1e-08)


def local(queries, positives, neg_ids, table, accum):
    ids, counts = dedup(neg_ids, table.shape[0])
    received = lax.all_to_all(ids, "own", split_axis=0, concat_axis=0, tiled=True)
    rows = lax.all_to_all(gather(received, table), "own", split_axis=0, concat_axis=0, tiled=True)
    query_grad, neg_grad = compute(queries, positives, rows, counts)
    arrived = lax.all_to_all(neg_grad, "own", split_axis=0, concat_axis=0, tiled=True)
    dense = scatter(received, arrived, table.shape[0])
    summed = lax.psum(dense, "dp")
    return (adagrad(table, accum, summed), query_grad)


def solution(mesh):
    return jax.shard_map(
        local,
        mesh=mesh,
        in_specs=(
            P(("dp", "own"), None),
            P(("dp", "own"), None),
            P(("dp", "own"), None),
            P("own", None),
            P("own", None),
        ),
        out_specs=(P("own", None), P(("dp", "own"), None)),
        check_vma=False,
    )
```

time: 629 us -> 262 us (0.42)
  matrix products: 290 us -> 0 us
  Pallas kernels: 0 us -> 86.8 us
  other arithmetic: 93.5 us -> 8.57 us
  waiting for transfers between devices: 134 us -> 74.6 us
  local copies, waits for them, and re-layouts: 32.1 us -> 5.6 us
  blocking collectives: 50.9 us -> 71.4 us
  starting transfers between devices: 12.3 us -> 0.04 us
    dot_general x12 -> x0, matrix products: 290 us -> none  [the longest x4 129 us: score_block(): neg_grad = jnp.dot(neg_dz.T, query_rows, precision=lax.Precision.HIGHEST)]
    pallas_call x0 -> x4, Pallas kernels: none -> 86.8 us  [the longest x1 51.3 us: compute(): pl.pallas_call(functools.partial(compute_kernel, tq), out_shape=(jax.Shap...]
    all_to_all x2 -> x0, waiting for transfers between devices: 58 us -> none  [the longest x1 51.6 us: local(): lax.all_to_all(jnp.take(table, local_ids.reshape(-1), axis=0).reshape(loc...]
    scatter-add x1 -> x0, other arithmetic: 46.5 us -> none  [local(): dense = jax.ops.segment_sum(flat_grads, local_ids, num_segments=rows_dev)]
    reduce_sum x8 -> x0, other arithmetic: 33 us -> none  [the longest x4 32.4 us: score_block(): total = pos_exp + jnp.sum(neg_exp, axis=1)]
    gather x1 -> x0, local copies, waits for them, and re-layouts: 30.1 us -> none  [local(): jnp.take(table, local_ids.reshape(-1), axis=0)]
    all_to_all x1 -> x3, blocking collectives: 50.9 us -> 71.4 us  [the longest x1 29.6 us: local(): lax.all_to_all(gather(received, table), 'own', split_axis=0, concat_axis=...]
    all_to_all x2 -> x0, starting transfers between devices: 12.3 us -> none  [the longest x1 7.58 us: local(): lax.all_to_all(neg_ids, 'own', split_axis=0, concat_axis=0, tiled=True)]
  transfers between devices with their start and end apart: 3 -> 1, of which waited for: 3 -> 1; matrix products, arithmetic and copies ran while one was open for 0% -> 0% of each run, Pallas kernels for 0% -> 0%
where the time goes in v1:
time: 262 us; the launch traced here: 261 us
  Pallas kernels  86.8 us (33%)
  waiting for transfers between devices  74.6 us (28%)
  blocking collectives  71.4 us (27%)
  between operations  14.1 us (5%)
  other arithmetic  8.57 us (3%)
  local copies, waits for them, and re-layouts  5.6 us (2%)
    psum x1, waiting for transfers between devices, local(): summed = lax.psum(dense, 'dp')  74.6 us
    pallas_call x1, Pallas kernels, compute(): pl.pallas_call(functools.partial(compute_kernel, tq), out_shape=(jax.Shap...  51.3 us
    all_to_all x1, blocking collectives, local(): lax.all_to_all(gather(received, table), 'own', split_axis=0, concat_axis=...  29.6 us
    all_to_all x1, blocking collectives, local(): lax.all_to_all(neg_grad, 'own', split_axis=0, concat_axis=0, tiled=True)  28 us
    pallas_call x1, Pallas kernels, scatter(): pl.pallas_call(scatter_kernel, out_shape=jax.ShapeDtypeStruct((rows_dev,...  17.6 us
    pallas_call x1, Pallas kernels, gather(): pl.pallas_call(gather_kernel, out_shape=jax.ShapeDtypeStruct((ids.shape[0...  14.1 us
    all_to_all x1, blocking collectives, local(): lax.all_to_all(ids, 'own', split_axis=0, concat_axis=0, tiled=True)  13.9 us
    sub x1, other arithmetic, adagrad(): return table_rows - 0.5 * grad / (jnp.sqrt(new_accum) + 1e-08)  8.57 us
  transfers between devices with their start and end apart: 1, of which 1 were waited for; matrix products, arithmetic and copies ran while one was open for 0% of the time, Pallas kernels for 0%

profile of v1, /device:TPU:1, one launch (start us, length us, event | category | flops | bytes accessed | tf_op | source)
XLA Modules:
  0.0 261.1 jit_solution(3946105051234083868)
XLA Ops:
  7.2 0.0 all-reduce.2.cloned.1.call-start
  7.2 0.0 copy-start.3
  7.2 0.7 copy-done.3
  8.0 3.9 %dedup.1 = (s32[16,8,128]{2,1,0:T(8,128)S(1)}, f32[16,8,256]{2,1,0:T(8,128)S(1)}) custom-call(s32[16,512]{1,0:T(8,128)S(1)} %copy-done.3), custom_call_target="tpu_custom_call" | custom-call | tf_op jit(solution)/shard_map/dedup/pallas_call | solution.py:71
  11.8 0.0 copy-start.2
  11.9 0.6 copy-done.2
  12.5 13.9 %all_to_all.15.ids_ref = s32[16,8,128]{2,1,0:T(8,128)S(1)} all-to-all(s32[16,8,128]{2,1,0:T(8,128)S(1)} %get-tuple-element.6), channel_id=1, replica_groups=mesh['dp'=8,'own'=16] {'own'}, dimensions={0} | all-to-all | bytes 131072 | tf_op jit(solution)/shard_map/all_to_all | solution.py:257
  26.4 0.0 copy-start.1
  26.4 2.2 copy-done.1
  28.6 14.1 %gather.1 = f32[16,256,128]{2,1,0:T(8,128)S(1)} custom-call(s32[16,8,128]{2,1,0:T(8,128)S(1)} %all_to_all.15.ids_ref, f32[8192,128]{1,0:T(8,128)S(1)} %copy-done.1), custom_call_target="tpu_custom_call" | custom-call | tf_op jit(solution)/shard_map/gather/pallas_call | solution.py:99
  42.7 29.6 %all_to_all.16.n_ref = f32[16,256,128]{2,1,0:T(8,128)} all-to-all(f32[16,256,128]{2,1,0:T(8,128)S(1)} %gather.1), channel_id=1, replica_groups=mesh['dp'=8,'own'=16] {'own'}, dimensions={0} | all-to-all | bytes 4194304 | tf_op jit(solution)/shard_map/all_to_all | solution.py:258
  72.2 51.3 %compute.1 = (f32[2048,128]{1,0:T(8,128)}, f32[16,256,128]{2,1,0:T(8,128)}) custom-call(f32[2048,128]{1,0:T(8,128)} %q_ref.1, f32[2048,128]{1,0:T(8,128)} %p_ref.1, f32[16,256,128]{2,1,0:T(8,128)} %all_to_all.16.n_ref, f32[16,8,256]{2,1,0:T(8,128)} %copy-done.2), custom_call_target="tpu_custom_call" | custom-call | tf_op jit(solution)/shard_map/compute/pallas_call | solution.py:239
  123.5 28.0 %all_to_all.17.grad_ref = f32[16,256,128]{2,1,0:T(8,128)S(1)} all-to-all(f32[16,256,128]{2,1,0:T(8,128)} %get-tuple-element.8), channel_id=1, replica_groups=mesh['dp'=8,'own'=16] {'own'}, dimensions={0} | all-to-all | bytes 4194304 | tf_op jit(solution)/shard_map/all_to_all | solution.py:260
  151.5 17.6 %scatter.1 = f32[8192,128]{1,0:T(8,128)S(1)} custom-call(s32[16,8,128]{2,1,0:T(8,128)S(1)} %all_to_all.15.ids_ref, f32[16,256,128]{2,1,0:T(8,128)S(1)} %all_to_all.17.grad_ref), custom_call_target="tpu_custom_call" | custom-call | tf_op jit(solution)/shard_map/scatter/pallas_call | solution.py:129
  169.1 0.0 copy-start
  169.1 2.0 copy-done
  171.1 0.0 all-reduce.2.cloned.1.call-update
  171.1 74.6 %all-reduce.2.cloned.1.call-done = f32[8192,128]{1,0:T(8,128)} async-done(((f32[8192,128]{1,0:T(8,128)}), f32[8192,128]{1,0:T(8,128)}) %all-reduce.2.cloned.1.call-update) | async-done | bytes 4194320 | tf_op jit(solution)/shard_map/psum | solution.py:262
  245.7 8.6 %divide_subtract_fusion = f32[8192,128]{1,0:T(8,128)} fusion(f32[8192,128]{1,0:T(8,128)} %table_ref.1, f32[8192,128]{1,0:T(8,128)} %param.9, f32[8192,128]{1,0:T(8,128)} %all-reduce.2.cloned.1.call-done), kind=kLoop, calls=%fused_computation | loop fusion | flops 6291456 | bytes 16777216 | tf_op jit(solution)/shard_map/sub | solution.py:252
Async XLA Ops:
  7.2 238.5 %all-reduce.2.cloned.1.call-start = ((), (), s32[]{:S(2)}) async-start(), calls=%async_computation.3 | async-start | bytes 8388608 | tf_op jit(solution)/shard_map/psum | solution.py:262
  7.2 0.8 copy-start.3
  11.8 0.7 copy-start.2
  26.4 2.2 copy-start.1
  169.1 2.0 copy-start
Sparse Core Ops, SparseCore 0:
  171.3 74.4 all-reduce.1

commit v2 on v1

--- a/solution.py
+++ b/solution.py
@@ -81,48 +81,19 @@
     )(ids)
 
 
-def gather_kernel(ids_ref, table_ref, out_ref):
-    few = out_ref.shape[1]
-
-    def block(s, c):
-        def group(g, c):
+def scatter_kernel(ids_ref, grad_ref, out_ref):
+    out_ref[...] = jnp.zeros_like(out_ref)
+
+    def block(k, c):
+        s, h = k // 2, k % 2
+        for b in range(8):
+            at = [pl.ds(ids_ref[s, h, b * 16 + i], 1) for i in range(16)]
+            vals = [out_ref[at[i], :] + grad_ref[s, pl.ds(h * 128 + b * 16 + i, 1), :] for i in range(16)]
             for i in range(16):
-                j = g * 16 + i
-                out_ref[s, pl.ds(j, 1), :] = table_ref[pl.ds(ids_ref[s, j >> 7, j & 127], 1), :]
-            return c
-        return lax.fori_loop(0, few // 16, group, c)
-
-    lax.fori_loop(0, out_ref.shape[0], block, 0)
-
-
-def gather(ids, table):
-    return pl.pallas_call(
-        gather_kernel,
-        out_shape=jax.ShapeDtypeStruct((ids.shape[0], 256, 128), F32),
-        in_specs=[pl.BlockSpec(memory_space=pltpu.SMEM), pl.BlockSpec(memory_space=pltpu.VMEM)],
-        out_specs=pl.BlockSpec(memory_space=pltpu.VMEM),
-        compiler_params=pltpu.CompilerParams(vmem_limit_bytes=32 * MIB),
-        name="gather",
-    )(ids, table)
-
-
-def scatter_kernel(ids_ref, grad_ref, out_ref):
-    few = grad_ref.shape[1]
-    out_ref[...] = jnp.zeros_like(out_ref)
-
-    def block(s, c):
-        def group(g, c):
-            at, vals = [], []
-            for i in range(16):
-                j = g * 16 + i
-                at.append(ids_ref[s, j >> 7, j & 127])
-                vals.append(out_ref[pl.ds(at[i], 1), :] + grad_ref[s, pl.ds(j, 1), :])
-            for i in range(16):
-                out_ref[pl.ds(at[i], 1), :] = vals[i]
-            return c
-        return lax.fori_loop(0, few // 16, group, c)
-
-    lax.fori_loop(0, grad_ref.shape[0], block, 0)
+                out_ref[at[i], :] = vals[i]
+        return c
+
+    lax.fori_loop(0, 2 * grad_ref.shape[0], block, 0)
 
 
 def scatter(ids, grads, rows_dev):
@@ -202,23 +173,6 @@
     return wc * (g1[:, 0:128] + (g1[:, 128:256] + g2))
 
 
-def compute_kernel(tq, q_ref, p_ref, n_ref, w_ref, qg_ref, g_ref, qtf, ptf, qt2, m, ms, total, qacc, eh, el):
-    prepare(q_ref, p_ref, qtf, ptf, qt2, m, total, qacc)
-
-    def a(s, c):
-        phase_a(n_ref[s], w_ref[s, 0:1, :], s, qt2, m, ms, total, qacc, eh, el, tq)
-        return c
-
-    lax.fori_loop(0, n_ref.shape[0], a, 0)
-    finish(qg_ref, ptf, m, total, qacc)
-
-    def b(s, c):
-        g_ref[s] = phase_b(w_ref[s, 0:1, :], s, qtf, m, ms, total, eh, el)
-        return c
-
-    lax.fori_loop(0, n_ref.shape[0], b, 0)
-
-
 def compute_scratch(count, owners):
     return [
         pltpu.VMEM((128, count), F32),
@@ -233,34 +187,305 @@
     ]
 
 
-def compute(q, p, n, w, tq=512):
-    count, owners = q.shape[0], n.shape[0]
+def exchange_kernel(
+    tq, ids_ref, cnt_ref, q_ref, p_ref, table_ref, qg_ref, idr_ref, arrived_ref,
+    qtf, ptf, qt2, m, ms, total, qacc, eh, el,
+    idr, ids_smem, sent, rows, gsent, wslot,
+    ids_s, ids_r, row_s, row_r, grad_s, grad_r, local_s,
+):
+    owners = ids_ref.shape[0]
+    me = lax.axis_index("own")
+    x, y = me // 4, me % 4
+
+    def up(s):
+        dx, dy = s % 4, (s + s // 4) % 4
+        return ((x + dx) % 4) * 4 + (y + dy) % 4
+
+    def down(s):
+        dx, dy = s % 4, (s + s // 4) % 4
+        return ((x + 4 - dx) % 4) * 4 + (y + 4 - dy) % 4
+
+    def remote(src, dst, send, recv, device):
+        return pltpu.make_async_remote_copy(
+            src_ref=src, dst_ref=dst, send_sem=send, recv_sem=recv,
+            device_id={"own": device}, device_id_type=pl.DeviceIdType.MESH,
+        )
+
+    def ids_copy(s):
+        return remote(ids_ref.at[up(s)], idr.at[s], ids_s.at[s], ids_r.at[s], up(s))
+
+    def row_copy(s):
+        return remote(sent.at[s], rows.at[s], row_s.at[s], row_r.at[s], down(s))
+
+    def grad_copy(s):
+        return remote(gsent.at[s], arrived_ref.at[s], grad_s.at[s], grad_r.at[s], up(s))
+
+    def each(first, body):
+        def step(s, c):
+            body(s)
+            return c
+
+        lax.fori_loop(first, owners, step, 0)
+
+    barrier = pltpu.get_barrier_semaphore()
+    each(1, lambda s: pl.semaphore_signal(
+        barrier, inc=1, device_id={"own": up(s)}, device_id_type=pl.DeviceIdType.MESH))
+    pl.semaphore_wait(barrier, owners - 1)
+    each(1, lambda s: ids_copy(s).start())
+    idr[0] = ids_ref[me]
+
+    def counts(s):
+        wslot[s] = cnt_ref[up(s)]
+
+    each(0, counts)
+    prepare(q_ref, p_ref, qtf, ptf, qt2, m, total, qacc)
+    each(1, lambda s: ids_copy(s).wait_recv())
+    to_smem = pltpu.make_async_copy(idr, ids_smem, local_s.at[0])
+    to_smem.start()
+    idr_ref[...] = idr[...]
+    to_smem.wait()
+
+    def fetch(s, into):
+        def half(h, c):
+            for i in range(128):
+                into[s, pl.ds(h * 128 + i, 1), :] = table_ref[pl.ds(ids_smem[s, h, i], 1), :]
+            return c
+
+        lax.fori_loop(0, 2, half, 0)
+
+    def send_rows(s):
+        fetch(s, sent)
+        row_copy(s).start()
+
+    each(1, send_rows)
+    fetch(0, rows)
+
+    def scores(s):
+        @pl.when(s > 0)
+        def _():
+            row_copy(s).wait_recv()
+
+        phase_a(rows[s], wslot[s, 0:1, :], s, qt2, m, ms, total, qacc, eh, el, tq)
+
+    each(0, scores)
+
+    def gradients(i):
+        s = (i + 1) % owners
+        gsent[s] = phase_b(wslot[s, 0:1, :], s, qtf, m, ms, total, eh, el)
+
+        @pl.when(s > 0)
+        def _():
+            grad_copy(s).start()
+
+    each(0, gradients)
+    own = pltpu.make_async_copy(gsent.at[0], arrived_ref.at[0], local_s.at[1])
+    own.start()
+    finish(qg_ref, ptf, m, total, qacc)
+    each(1, lambda s: ids_copy(s).wait_send())
+    each(1, lambda s: row_copy(s).wait_send())
+    each(1, lambda s: grad_copy(s).wait())
+    own.wait()
+
+
+def exchange(ids, counts, q, p, table, tq=512):
+    count, owners = q.shape[0], ids.shape[0]
     vm = pl.BlockSpec(memory_space=pltpu.VMEM)
+    dma = pltpu.SemaphoreType.DMA((owners,))
     return pl.pallas_call(
-        functools.partial(compute_kernel, tq),
-        out_shape=(jax.ShapeDtypeStruct((count, 128), F32), jax.ShapeDtypeStruct((owners, 256, 128), F32)),
-        in_specs=[vm] * 4,
-        out_specs=(vm, vm),
-        scratch_shapes=compute_scratch(count, owners),
-        compiler_params=pltpu.CompilerParams(vmem_limit_bytes=60 * MIB),
-        name="compute",
-    )(q, p, n, w)
-
-
-def adagrad(table_rows, accum_rows, grad):
-    new_accum = accum_rows + grad * grad
-    return table_rows - 0.5 * grad / (jnp.sqrt(new_accum) + 1e-08)
+        functools.partial(exchange_kernel, tq),
+        out_shape=(
+            jax.ShapeDtypeStruct((count, 128), F32),
+            jax.ShapeDtypeStruct(ids.shape, I32),
+            jax.ShapeDtypeStruct((owners, 256, 128), F32),
+        ),
+        in_specs=[vm] * 5,
+        out_specs=(vm, vm, pl.BlockSpec(memory_space=pl.ANY)),
+        scratch_shapes=compute_scratch(count, owners)
+        + [
+            pltpu.VMEM(ids.shape, I32),
+            pltpu.SMEM(ids.shape, I32),
+            pltpu.VMEM((owners, 256, 128), F32),
+            pltpu.VMEM((owners, 256, 128), F32),
+            pltpu.VMEM((owners, 256, 128), F32),
+            pltpu.VMEM(counts.shape, F32),
+        ]
+        + [dma] * 6
+        + [pltpu.SemaphoreType.DMA((2,))],
+        compiler_params=pltpu.CompilerParams(
+            vmem_limit_bytes=60 * MIB, collective_id=0, has_side_effects=True
+        ),
+        name="exchange",
+    )(ids, counts, q, p, table)
+
+
+def update_kernel(
+    d_ref, table_ref, accum_ref, out_ref,
+    mine, other, ring, fresh, tab, acc,
+    load_s, core_s, core_r, ring_s, ring_r, all_s, all_r, peer_s, peer_r,
+):
+    rows = d_ref.shape[0]
+    half, ch = rows // 2, rows // 8
+    hf = ch // 2
+    dp = lax.axis_index("dp")
+    z, c = dp // 2, dp % 2
+    peer = z * 2 + (1 - c)
+    nxt = ((z + 1) % 4) * 2 + c
+    prv = ((z + 3) % 4) * 2 + c
+
+    def remote(src, dst, send, recv, device):
+        return pltpu.make_async_remote_copy(
+            src_ref=src, dst_ref=dst, send_sem=send, recv_sem=recv,
+            device_id={"dp": device}, device_id_type=pl.DeviceIdType.MESH,
+        )
+
+    def at(k, core, part=None):
+        first = core * half + ((z + k) % 4) * ch
+        if part is None:
+            return pl.ds(pl.multiple_of(first, ch), ch)
+        return pl.ds(pl.multiple_of(first + part * hf, hf), hf)
+
+    loads = [pltpu.make_async_copy(d_ref.at[at(k, c)], mine.at[k], load_s.at[k]) for k in range(4)]
+    loads.append(pltpu.make_async_copy(table_ref.at[at(0, c)], tab, load_s.at[4]))
+    loads.append(pltpu.make_async_copy(accum_ref.at[at(0, c)], acc, load_s.at[5]))
+    for k in (2, 1, 3, 0, 4, 5):
+        loads[k].start()
+
+    barrier = pltpu.get_barrier_semaphore()
+    for device in (peer, nxt, prv):
+        pl.semaphore_signal(barrier, inc=1, device_id={"dp": device}, device_id_type=pl.DeviceIdType.MESH)
+    pl.semaphore_wait(barrier, 3)
+
+    core = [remote(d_ref.at[at(k, 1 - c)], other.at[k], core_s.at[k], core_r.at[k], peer) for k in range(4)]
+    for k in (2, 1, 3, 0):
+        core[k].start()
+
+    def pair(k):
+        loads[k].wait()
+        core[k].wait_recv()
+        mine[k] = mine[k] + other[k]
+
+    first, second = pl.ds(0, hf), pl.ds(hf, hf)
+
+    def hop(i, k, part, device):
+        return remote(mine.at[k, part], ring.at[i], ring_s.at[i], ring_r.at[i], device)
+
+    hops = [
+        hop(0, 2, first, nxt), hop(1, 2, second, prv),
+        hop(2, 1, second, nxt), hop(3, 3, first, prv),
+        hop(4, 1, first, nxt), hop(5, 3, second, prv),
+    ]
+    pair(2)
+    hops[0].start()
+    hops[1].start()
+    pair(1)
+    hops[2].start()
+    pair(3)
+    hops[3].start()
+    hops[0].wait_recv()
+    mine[1, first, :] = mine[1, first, :] + ring[0]
+    hops[4].start()
+    hops[1].wait_recv()
+    mine[3, second, :] = mine[3, second, :] + ring[1]
+    hops[5].start()
+    pair(0)
+    loads[4].wait()
+    loads[5].wait()
+
+    def adagrad(part, a, b):
+        grad = mine[0, part, :] + (ring[a] + ring[b])
+        new_accum = acc[part, :] + grad * grad
+        fresh[part, :] = tab[part, :] - 0.5 * grad / (jnp.sqrt(new_accum) + 1e-08)
+
+    def own_part(i, part, device):
+        rows_ = at(0, c, part)
+        return remote(fresh.at[pl.ds(part * hf, hf)], out_ref.at[rows_], all_s.at[i], all_r.at[i], device)
+
+    def passed(i, k, part, device):
+        rows_ = at(k, c, part)
+        return remote(out_ref.at[rows_], out_ref.at[rows_], all_s.at[i], all_r.at[i], device)
+
+    def to_peer(k, part):
+        rows_ = at(k, c, part)
+        src = fresh.at[pl.ds(part * hf, hf)] if k == 0 else out_ref.at[rows_]
+        return remote(src, out_ref.at[rows_], peer_s.at[k, part], peer_r.at[k, part], peer)
+
+    shares = [
+        own_part(0, 0, nxt), own_part(1, 1, nxt), own_part(2, 0, prv), own_part(3, 1, prv),
+        passed(4, 3, 0, nxt), passed(5, 1, 1, prv),
+    ]
+    peers = [[to_peer(k, part) for part in range(2)] for k in range(4)]
+    keep = [
+        pltpu.make_async_copy(fresh.at[pl.ds(part * hf, hf)], out_ref.at[at(0, c, part)], load_s.at[6 + part])
+        for part in range(2)
+    ]
+    hops[3].wait_recv()
+    hops[4].wait_recv()
+    adagrad(first, 3, 4)
+    shares[0].start()
+    hops[2].wait_recv()
+    hops[5].wait_recv()
+    adagrad(second, 2, 5)
+    shares[3].start()
+    shares[1].start()
+    shares[2].start()
+    for part in range(2):
+        peers[0][part].start()
+        keep[part].start()
+    shares[0].wait_recv()
+    shares[4].start()
+    peers[3][0].start()
+    shares[3].wait_recv()
+    shares[5].start()
+    peers[1][1].start()
+    shares[1].wait_recv()
+    peers[3][1].start()
+    shares[2].wait_recv()
+    peers[1][0].start()
+    shares[4].wait_recv()
+    peers[2][0].start()
+    shares[5].wait_recv()
+    peers[2][1].start()
+    for k in range(4):
+        for part in range(2):
+            peers[k][part].wait()
+    for copy in core + hops + shares:
+        copy.wait_send()
+    for copy in keep:
+        copy.wait()
+
+
+def update(dense, table, accum):
+    rows = dense.shape[0]
+    ch = rows // 8
+    hbm = pl.BlockSpec(memory_space=pl.ANY)
+    dma = pltpu.SemaphoreType.DMA
+    return pl.pallas_call(
+        update_kernel,
+        out_shape=jax.ShapeDtypeStruct((rows, 128), F32),
+        in_specs=[hbm] * 3,
+        out_specs=hbm,
+        scratch_shapes=[
+            pltpu.VMEM((4, ch, 128), F32),
+            pltpu.VMEM((4, ch, 128), F32),
+            pltpu.VMEM((6, ch // 2, 128), F32),
+            pltpu.VMEM((ch, 128), F32),
+            pltpu.VMEM((ch, 128), F32),
+            pltpu.VMEM((ch, 128), F32),
+            dma((8,)), dma((4,)), dma((4,)), dma((6,)), dma((6,)), dma((6,)), dma((6,)),
+            dma((4, 2)), dma((4, 2)),
+        ],
+        compiler_params=pltpu.CompilerParams(
+            vmem_limit_bytes=24 * MIB, collective_id=1, has_side_effects=True
+        ),
+        name="update",
+    )(dense, table, accum)
 
 
 def local(queries, positives, neg_ids, table, accum):
     ids, counts = dedup(neg_ids, table.shape[0])
-    received = lax.all_to_all(ids, "own", split_axis=0, concat_axis=0, tiled=True)
-    rows = lax.all_to_all(gather(received, table), "own", split_axis=0, concat_axis=0, tiled=True)
-    query_grad, neg_grad = compute(queries, positives, rows, counts)
-    arrived = lax.all_to_all(neg_grad, "own", split_axis=0, concat_axis=0, tiled=True)
+    query_grad, received, arrived = exchange(ids, counts, queries, positives, table)
     dense = scatter(received, arrived, table.shape[0])
-    summed = lax.psum(dense, "dp")
-    return (adagrad(table, accum, summed), query_grad)
+    return (update(dense, table, accum), query_grad)
 
 
 def solution(mesh):

time: 262 us -> 156 us (0.60)
  waiting for transfers between devices: 74.6 us -> 0 us
  blocking collectives: 71.4 us -> 0 us
  Pallas kernels: 86.8 us -> 145 us
  between operations: 14.1 us -> 0.71 us
  other arithmetic: 8.57 us -> 0 us
  local copies, waits for them, and re-layouts: 5.6 us -> 9.93 us
    psum x1 -> x0, waiting for transfers between devices: 74.6 us -> none  [local(): summed = lax.psum(dense, 'dp')]
    all_to_all x3 -> x0, blocking collectives: 71.4 us -> none  [the longest x1 29.6 us: local(): lax.all_to_all(gather(received, table), 'own', split_axis=0, concat_axis=...]
    pallas_call x2, Pallas kernels: 65.4 us -> 134 us  [the longest x1 87.5 us: exchange(): pl.pallas_call(functools.partial(exchange_kernel, tq), out_shape=(jax.Sha...]
    pallas_call x1, Pallas kernels: 17.6 us -> 7.42 us  [scatter(): pl.pallas_call(scatter_kernel, out_shape=jax.ShapeDtypeStruct((rows_dev,...]
    sub x1 -> x0, other arithmetic: 8.57 us -> none  [adagrad(): return table_rows - 0.5 * grad / (jnp.sqrt(new_accum) + 1e-08)]
    unnamed x8 -> x18, local copies, waits for them, and re-layouts: 5.6 us -> 9.93 us
  transfers between devices with their start and end apart: 1 -> 0, of which waited for: 1 -> 0; matrix products, arithmetic and copies ran while one was open for 0% -> 0% of each run, Pallas kernels for 0% -> 0%
where the time goes in v2:
time: 156 us
  Pallas kernels  145 us (93%)
  local copies, waits for them, and re-layouts  9.93 us (6%)
    pallas_call x1, Pallas kernels, exchange(): pl.pallas_call(functools.partial(exchange_kernel, tq), out_shape=(jax.Sha...  87.5 us
    pallas_call x1, Pallas kernels, update(): pl.pallas_call(update_kernel, out_shape=jax.ShapeDtypeStruct((rows, 128),...  46.2 us
    unnamed x18, local copies, waits for them, and re-layouts  9.93 us
    pallas_call x1, Pallas kernels, scatter(): pl.pallas_call(scatter_kernel, out_shape=jax.ShapeDtypeStruct((rows_dev,...  7.42 us
    pallas_call x1, Pallas kernels, dedup(): pl.pallas_call(functools.partial(dedup_kernel, rows_dev), out_shape=(jax....  3.88 us

profile of v2, /device:TPU:1, one launch (start us, length us, event | category | flops | bytes accessed | tf_op | source)
XLA Modules:
  0.0 155.6 jit_solution(13548612394688529186)
XLA Ops:
  0.6 0.0 copy-start.6
  0.6 0.7 copy-done.6
  1.4 3.9 %dedup.1 = (s32[16,8,128]{2,1,0:T(8,128)S(1)}, f32[16,8,256]{2,1,0:T(8,128)S(1)}) custom-call(s32[16,512]{1,0:T(8,128)S(1)} %copy-done.6), custom_call_target="tpu_custom_call" | custom-call | tf_op jit(solution)/shard_map/dedup/pallas_call | solution.py:71
  5.3 0.0 copy-start.3
  5.3 0.7 copy-done.3
  5.9 0.0 copy-start.4
  5.9 0.6 copy-done.4
  6.6 87.5 %exchange.1 = (f32[2048,128]{1,0:T(8,128)}, s32[16,8,128]{2,1,0:T(8,128)}, f32[16,256,128]{2,1,0:T(8,128)}) custom-call(s32[16,8,128]{2,1,0:T(8,128)} %copy-done.4, f32[16,8,256]{2,1,0:T(8,128)} %copy-done.3, f32[2048,128]{1,0:T(8,128)} %q_ref.1, f32[2048,128]{1,0:T(8,128)} %p_ref.1, f32[8192,128]{1,0:T(8,128)} %table_ref.3), custom_call_target="tpu_custom_call" | custom-call | tf_op jit(solution)/shard_map/exchange/pallas_call | solution.py:294
  94.1 0.0 copy-start
  94.1 0.0 copy-start.2
  94.1 1.7 %copy-done.2 = f32[16,256,128]{2,1,0:T(8,128)S(1)} copy-done((f32[16,256,128]{2,1,0:T(8,128)S(1)}, f32[16,256,128]{2,1,0:T(8,128)}, u32[]{:S(2)}) %copy-start.2) | copy-done | bytes 2097176
  95.8 0.0 copy-start.5
  95.8 1.0 copy-done.5
  96.8 7.4 %scatter.1.d_ref = f32[8192,128]{1,0:T(8,128)S(1)} custom-call(s32[16,8,128]{2,1,0:T(8,128)S(1)} %copy-done.5, f32[16,256,128]{2,1,0:T(8,128)S(1)} %copy-done.2), custom_call_target="tpu_custom_call" | custom-call | tf_op jit(solution)/shard_map/scatter/pallas_call | solution.py:100
  104.3 0.0 copy-done
  104.3 0.0 copy-start.1
  104.3 2.2 %copy-done.1 = f32[8192,128]{1,0:T(8,128)S(1)} copy-done((f32[8192,128]{1,0:T(8,128)S(1)}, f32[8192,128]{1,0:T(8,128)}, u32[]{:S(2)}) %copy-start.1) | copy-done | bytes 4194328
  106.5 46.2 %update.1 = f32[8192,128]{1,0:T(8,128)S(1)} custom-call(f32[8192,128]{1,0:T(8,128)S(1)} %scatter.1.d_ref, f32[8192,128]{1,0:T(8,128)S(1)} %copy-done, f32[8192,128]{1,0:T(8,128)S(1)} %copy-done.1), custom_call_target="tpu_custom_call" | custom-call | tf_op jit(solution)/shard_map/update/pallas_call | solution.py:462
  152.6 0.0 copy-start.7
  152.7 2.0 %copy.9 = f32[8192,128]{1,0:T(8,128)} copy(f32[8192,128]{1,0:T(8,128)S(1)} %update.1) | data formatting | bytes 8388608
  154.7 0.0 copy-done.7
  154.7 1.0 copy.10
Async XLA Ops:
  0.6 0.8 copy-start.6
  5.3 0.7 copy-start.3
  5.9 0.6 copy-start.4
  94.1 10.2 %copy-start = (f32[8192,128]{1,0:T(8,128)S(1)}, f32[8192,128]{1,0:T(8,128)}, u32[]{:S(2)}) copy-start(f32[8192,128]{1,0:T(8,128)} %table_ref.3) | copy-start | bytes 12582916
  94.1 1.7 %copy-start.2 = (f32[16,256,128]{2,1,0:T(8,128)S(1)}, f32[16,256,128]{2,1,0:T(8,128)}, u32[]{:S(2)}) copy-start(f32[16,256,128]{2,1,0:T(8,128)} %get-tuple-element.10.grad_ref) | copy-start | bytes 6291460
  95.8 1.0 copy-start.5
  104.3 2.2 %copy-start.1 = (f32[8192,128]{1,0:T(8,128)S(1)}, f32[8192,128]{1,0:T(8,128)}, u32[]{:S(2)}) copy-start(f32[8192,128]{1,0:T(8,128)} %accum_ref.1) | copy-start | bytes 12582916
  152.6 2.0 %copy-start.7 = (f32[2048,128]{1,0:T(8,128)S(1)}, f32[2048,128]{1,0:T(8,128)}, u32[]{:S(2)}) copy-start(f32[2048,128]{1,0:T(8,128)} %get-tuple-element.15) | copy-start | bytes 3145732

commit v3 on v2

v3 whole, which is shorter than its diff:
```python
import functools
import jax
import jax.numpy as jnp
from jax import lax
from jax.experimental import pallas as pl
from jax.experimental.pallas import tpu as pltpu
from jax.sharding import PartitionSpec as P

F32, BF16, I32 = jnp.float32, jnp.bfloat16, jnp.int32
LOG2E = 1.4426950408889634
MIB = 1024 * 1024
UPDATE_VMEM = 52
SCATTER_VMEM = 55


def split(x):
    hi = x.astype(BF16)
    return hi, (x - hi.astype(F32)).astype(BF16)


def dot(a, b):
    return lax.dot_general(a, b, (((1,), (0,)), ((), ())), preferred_element_type=F32)


def dot_t(a, b):
    return lax.dot_general(a, b, (((1,), (1,)), ((), ())), preferred_element_type=F32)


def dedup(rows_dev, ids_ref, out_ref, cnt_ref):
    owners, per = ids_ref.shape
    few = 256
    base = lax.broadcasted_iota(I32, (owners, per), 0) * rows_dev
    local = (ids_ref[...] - base).astype(F32)
    cols = jnp.transpose(jnp.concatenate([local, jnp.zeros((128 - owners, per), F32)], axis=0))
    lane = lax.broadcasted_iota(I32, (128, per), 1)
    sub = lax.broadcasted_iota(I32, (128, per), 0)
    firsts, counts = [], []
    for r in range(owners):
        row = local[r : r + 1, :]
        count = jnp.zeros((1, per), F32)
        before = jnp.zeros((1, per), F32)
        for b in range(per // 128):
            col = cols[b * 128 : (b + 1) * 128, r : r + 1]
            eq = jnp.where(col == row, 1.0, 0.0)
            count = count + jnp.sum(eq, axis=0, keepdims=True)
            before = before + jnp.sum(jnp.where(sub + b * 128 < lane, eq, 0.0), axis=0, keepdims=True)
        firsts.append(before < 0.5)
        counts.append(count)
    first = jnp.concatenate([jnp.where(f, 1.0, 0.0) for f in firsts], axis=0)
    count = jnp.concatenate(counts, axis=0)
    tri = jnp.where(
        lax.broadcasted_iota(I32, (per, per), 0) < lax.broadcasted_iota(I32, (per, per), 1), 1.0, 0.0
    ).astype(BF16)
    place = dot(first.astype(BF16), tri)
    place = jnp.where(first > 0.5, place, -1.0).astype(I32)
    li = local.astype(I32)
    ci = count.astype(I32)
    parts = [(li >> 7).astype(F32), (li & 127).astype(F32), (ci >> 4).astype(F32), (ci & 15).astype(F32)]
    slot = lax.broadcasted_iota(I32, (few, per), 0)
    for r in range(owners):
        hot = jnp.where(slot == place[r : r + 1, :], 1.0, 0.0).astype(BF16)
        vals = jnp.concatenate([p[r : r + 1, :] for p in parts] + [jnp.zeros((12, per), F32)], axis=0)
        got = dot_t(vals.astype(BF16), hot)
        ids = got[0:1, :] * 128.0 + got[1:2, :]
        cnt = got[2:3, :] * 16.0 + got[3:4, :]
        both = jnp.concatenate([ids[:, :128], ids[:, 128:], jnp.zeros((6, 128), F32)], axis=0)
        out_ref[r] = jnp.clip(both.astype(I32), 0, rows_dev - 1)
        cnt_ref[r] = jnp.broadcast_to(cnt, (8, few))


def scatter_kernel(ids_ref, grad_hbm, out_ref, grad_ref, sems):
    owners = grad_hbm.shape[0]

    def load(s):
        return pltpu.make_async_copy(grad_hbm.at[s], grad_ref.at[s], sems.at[s])

    def start(s, c):
        load(s).start()
        return c

    lax.fori_loop(0, owners, start, 0)
    out_ref[...] = jnp.zeros_like(out_ref)

    def half(s, h):
        for b in range(8):
            at = [pl.ds(ids_ref[s, h, b * 16 + i], 1) for i in range(16)]
            vals = [out_ref[at[i], :] + grad_ref[s, pl.ds(h * 128 + b * 16 + i, 1), :] for i in range(16)]
            for i in range(16):
                out_ref[at[i], :] = vals[i]

    def block(s, c):
        load(s).wait()
        lax.fori_loop(0, 2, lambda h, c: (half(s, h), c)[1], c)
        return c

    lax.fori_loop(0, owners, block, 0)


def scatter(ids, grads, rows_dev):
    return pl.pallas_call(
        scatter_kernel,
        out_shape=jax.ShapeDtypeStruct((rows_dev, 128), F32),
        in_specs=[pl.BlockSpec(memory_space=pltpu.SMEM), pl.BlockSpec(memory_space=pl.ANY)],
        out_specs=pl.BlockSpec(memory_space=pltpu.VMEM),
        scratch_shapes=[pltpu.VMEM(grads.shape, F32), pltpu.SemaphoreType.DMA((grads.shape[0],))],
        compiler_params=pltpu.CompilerParams(vmem_limit_bytes=SCATTER_VMEM * MIB),
        name="scatter",
    )(ids, grads)


def prepare(q_ref, p_ref, qtf, ptf, qt2, m, total, qacc):
    count = q_ref.shape[0]
    for t in range(count // 128):
        tile = pl.ds(t * 128, 128)
        qt = jnp.transpose(q_ref[tile, :])
        pt = jnp.transpose(p_ref[tile, :])
        qtf[:, tile] = qt
        ptf[:, tile] = pt
        hi, lo = split(qt * LOG2E)
        qt2[0:128, tile] = hi
        qt2[128:256, tile] = lo
        m[0:1, tile] = jnp.sum(qt * pt, axis=0, keepdims=True) * LOG2E
    total[...] = jnp.ones_like(total)
    qacc[...] = ptf[...]


def right_side(n):
    hi, lo = split(n)
    return jnp.concatenate([hi, hi], axis=1), jnp.concatenate([lo, lo], axis=1)


def left_side(n, w):
    nth, ntl = split(jnp.transpose(n) * w)
    wh, wl = split(w)
    sub = lax.broadcasted_iota(I32, (16, 256), 0)
    wrows = jnp.where(sub == 0, wh.astype(F32), jnp.where(sub == 1, wl.astype(F32), 0.0)).astype(BF16)
    return jnp.concatenate([nth, wrows, ntl], axis=0)


def score_tile(sides, tile, qt2, score, peak):
    right = qt2[:, tile]
    sc = dot(sides[0], right) + dot(sides[1], right)
    score[:, tile] = sc
    peak[0:1, tile] = jnp.max(sc, axis=0, keepdims=True)


def soft_tile(left, tile, s, score, peak, m, ms, total, qacc, eh, el):
    old = m[0:1, tile]
    new = jnp.maximum(old, peak[0:1, tile])
    alpha = jnp.exp2(old - new)
    m[0:1, tile] = new
    ms[s, 0:1, tile] = new
    h, l = split(jnp.exp2(score[:, tile] - new))
    eh[s, :, tile] = h
    el[s, :, tile] = l
    a1 = dot(left, h)
    a2 = dot(left[0:144], l)
    total[0:1, tile] = total[0:1, tile] * alpha + (a1[128:129] + a1[129:130]) + (a2[128:129] + a2[129:130])
    qacc[:, tile] = qacc[:, tile] * alpha + (a1[0:128] + (a1[144:272] + a2[0:128]))


def finish(qg_ref, ptf, m, total, qacc):
    count = qacc.shape[1]
    for t in range(count // 128):
        tile = pl.ds(t * 128, 128)
        g = qacc[:, tile] * (1.0 / total[0:1, tile]) - ptf[:, tile]
        qg_ref[tile, :] = jnp.transpose(g)


def phase_b(w, s, qtf, m, ms, total, eh, el):
    c = jnp.exp2(ms[s, 0:1, :] - m[0:1, :]) * (1.0 / total[0:1, :])
    qh, ql = split(qtf[...] * c)
    g1 = dot_t(eh[s], jnp.concatenate([qh, ql], axis=0))
    g2 = dot_t(el[s], qh)
    wc = jnp.transpose(jnp.broadcast_to(w, (128, 256)))
    return wc * (g1[:, 0:128] + (g1[:, 128:256] + g2))


def exchange_kernel(
    tq, raw_ref, q_hbm, p_hbm, table_hbm, accum_hbm,
    qg_ref, idr_ref, arrived_ref, tab_ref, acc_ref,
    ids_ref, cnt_ref, q_ref, p_ref, table_ref,
    qtf, ptf, qt2, m, ms, total, qacc, eh, el, score_a, score_b, peak_a, peak_b,
    idr, ids_smem, sent, rows, gsent, wslot,
    ids_s, ids_r, row_s, row_r, grad_s, grad_r, local_s,
):
    owners = raw_ref.shape[0]
    me = lax.axis_index("own")
    x, y = me // 4, me % 4

    def up(s):
        dx, dy = s % 4, (s + s // 4) % 4
        return ((x + dx) % 4) * 4 + (y + dy) % 4

    def down(s):
        dx, dy = s % 4, (s + s // 4) % 4
        return ((x + 4 - dx) % 4) * 4 + (y + 4 - dy) % 4

    def remote(src, dst, send, recv, device):
        return pltpu.make_async_remote_copy(
            src_ref=src, dst_ref=dst, send_sem=send, recv_sem=recv,
            device_id={"own": device}, device_id_type=pl.DeviceIdType.MESH,
        )

    def ids_copy(s):
        return remote(ids_ref.at[up(s)], idr.at[s], ids_s.at[s], ids_r.at[s], up(s))

    def row_copy(s):
        return remote(sent.at[s], rows.at[s], row_s.at[s], row_r.at[s], down(s))

    def grad_copy(s):
        return remote(gsent.at[s], arrived_ref.at[s], grad_s.at[s], grad_r.at[s], up(s))

    def each(first, body):
        def step(s, c):
            body(s)
            return c

        lax.fori_loop(first, owners, step, 0)

    load_q = pltpu.make_async_copy(q_hbm, q_ref, local_s.at[2])
    load_p = pltpu.make_async_copy(p_hbm, p_ref, local_s.at[3])
    load_table = pltpu.make_async_copy(table_hbm, table_ref, local_s.at[4])
    dp, ch = lax.axis_index("dp"), tab_ref.shape[0]
    share = pl.ds(pl.multiple_of((dp % 2 * 4 + dp // 2) * ch, ch), ch)
    keep_tab = pltpu.make_async_copy(table_hbm.at[share], tab_ref, local_s.at[5])
    keep_acc = pltpu.make_async_copy(accum_hbm.at[share], acc_ref, local_s.at[6])
    load_q.start()
    load_p.start()
    load_table.start()
    barrier = pltpu.get_barrier_semaphore()
    each(1, lambda s: pl.semaphore_signal(
        barrier, inc=1, device_id={"own": up(s)}, device_id_type=pl.DeviceIdType.MESH))
    dedup(table_ref.shape[0], raw_ref, ids_ref, cnt_ref)
    pl.semaphore_wait(barrier, owners - 1)
    each(1, lambda s: ids_copy(s).start())
    idr[0] = ids_ref[me]

    def counts(s):
        wslot[s] = cnt_ref[up(s)]

    each(0, counts)
    load_q.wait()
    load_p.wait()
    prepare(q_ref, p_ref, qtf, ptf, qt2, m, total, qacc)
    load_table.wait()
    each(1, lambda s: ids_copy(s).wait_recv())
    to_smem = pltpu.make_async_copy(idr, ids_smem, local_s.at[0])
    to_smem.start()
    idr_ref[...] = idr[...]
    to_smem.wait()

    def fetch(s, into):
        def half(h, c):
            for i in range(128):
                into[s, pl.ds(h * 128 + i, 1), :] = table_ref[pl.ds(ids_smem[s, h, i], 1), :]
            return c

        lax.fori_loop(0, 2, half, 0)

    def send_rows(s):
        fetch(s, sent)
        row_copy(s).start()

    each(1, send_rows)
    fetch(0, rows)
    keep_tab.start()
    keep_acc.start()
    sums = (m, ms, total, qacc, eh, el)
    tiles = [pl.ds(t * tq, tq) for t in range(q_ref.shape[0] // tq)]

    def both(s, score, peak, score_before, peak_before):
        row_copy(s).wait_recv()
        sides = right_side(rows[s])
        left = left_side(rows[s - 1], wslot[s - 1, 0:1, :])
        for tile in tiles:
            score_tile(sides, tile, qt2, score, peak)
            soft_tile(left, tile, s - 1, score_before, peak_before, *sums)

    own_sides = right_side(rows[0])
    for tile in tiles:
        score_tile(own_sides, tile, qt2, score_a, peak_a)

    def two(i, c):
        both(2 * i + 1, score_b, peak_b, score_a, peak_a)

        both(2 * i + 2, score_a, peak_a, score_b, peak_b)
        return c

    lax.fori_loop(0, owners // 2 - 1, two, 0)
    both(owners - 1, score_b, peak_b, score_a, peak_a)
    last = left_side(rows[owners - 1], wslot[owners - 1, 0:1, :])
    for tile in tiles:
        soft_tile(last, tile, owners - 1, score_b, peak_b, *sums)

    def gradients(i):
        s = (i + 1) % owners
        gsent[s] = phase_b(wslot[s, 0:1, :], s, qtf, m, ms, total, eh, el)

        @pl.when(s > 0)
        def _():
            grad_copy(s).start()

    each(0, gradients)
    own = pltpu.make_async_copy(gsent.at[0], arrived_ref.at[0], local_s.at[1])
    own.start()
    finish(qg_ref, ptf, m, total, qacc)
    each(1, lambda s: ids_copy(s).wait_send())
    each(1, lambda s: row_copy(s).wait_send())
    each(1, lambda s: grad_copy(s).wait())
    own.wait()
    keep_tab.wait()
    keep_acc.wait()


def exchange(ids, q, p, table, accum, tq=512):
    count, owners = q.shape[0], ids.shape[0]
    vm = pl.BlockSpec(memory_space=pltpu.VMEM)
    hbm = pl.BlockSpec(memory_space=pl.ANY)
    dma = pltpu.SemaphoreType.DMA((owners,))
    return pl.pallas_call(
        functools.partial(exchange_kernel, tq),
        out_shape=(
            jax.ShapeDtypeStruct((count, 128), F32),
            jax.ShapeDtypeStruct((owners, 8, 128), I32),
            jax.ShapeDtypeStruct((owners, 256, 128), F32),
            jax.ShapeDtypeStruct((table.shape[0] // 8, 128), F32),
            jax.ShapeDtypeStruct((table.shape[0] // 8, 128), F32),
        ),
        in_specs=[vm, hbm, hbm, hbm, hbm],
        out_specs=(vm, vm, hbm, hbm, hbm),
        scratch_shapes=[
            pltpu.VMEM((owners, 8, 128), I32),
            pltpu.VMEM((owners, 8, 256), F32),
            pltpu.VMEM((count, 128), F32),
            pltpu.VMEM((count, 128), F32),
            pltpu.VMEM(table.shape, F32),
            pltpu.VMEM((128, count), F32),
            pltpu.VMEM((128, count), F32),
            pltpu.VMEM((256, count), BF16),
            pltpu.VMEM((8, count), F32),
            pltpu.VMEM((owners, 8, count), F32),
            pltpu.VMEM((8, count), F32),
            pltpu.VMEM((128, count), F32),
            pltpu.VMEM((owners, 256, count), BF16),
            pltpu.VMEM((owners, 256, count), BF16),
            pltpu.VMEM((256, count), F32),
            pltpu.VMEM((256, count), F32),
            pltpu.VMEM((8, count), F32),
            pltpu.VMEM((8, count), F32),
            pltpu.VMEM((owners, 8, 128), I32),
            pltpu.SMEM((owners, 8, 128), I32),
            pltpu.VMEM((owners, 256, 128), F32),
            pltpu.VMEM((owners, 256, 128), F32),
            pltpu.VMEM((owners, 256, 128), F32),
            pltpu.VMEM((owners, 8, 256), F32),
        ]
        + [dma] * 6
        + [pltpu.SemaphoreType.DMA((7,))],
        compiler_params=pltpu.CompilerParams(
            vmem_limit_bytes=61 * MIB, collective_id=0, has_side_effects=True
        ),
        name="exchange",
    )(ids, q, p, table, accum)


def update_kernel(
    subs, d_ref, tab, acc, out_ref,
    mine, other, ring, fresh,
    load_s, core_s, core_r, ring_s, ring_r, all_s, all_r, peer_s, peer_r,
):
    rows = d_ref.shape[0]
    half, ch = rows // 2, rows // 8
    hf = ch // 2
    sz = hf // subs
    dp = lax.axis_index("dp")
    z, c = dp // 2, dp % 2
    peer = z * 2 + (1 - c)
    nxt = ((z + 1) % 4) * 2 + c
    prv = ((z + 3) % 4) * 2 + c

    def remote(src, dst, send, recv, device):
        return pltpu.make_async_remote_copy(
            src_ref=src, dst_ref=dst, send_sem=send, recv_sem=recv,
            device_id={"dp": device}, device_id_type=pl.DeviceIdType.MESH,
        )

    def at(k, core, part, j):
        first = core * half + ((z + k) % 4) * ch + part * hf + j * sz
        return pl.ds(pl.multiple_of(first, sz), sz)

    def rows_of(part, j):
        return pl.ds(part * hf + j * sz, sz)

    span = range(subs)
    pieces = [(2, 0), (2, 1), (1, 1), (3, 0), (1, 0), (3, 1), (0, 0), (0, 1)]
    order = [(k, part, j) for k, part in pieces for j in span]
    loads, core = {}, {}
    for n, (k, part, j) in enumerate(order):
        loads[k, part, j] = pltpu.make_async_copy(
            d_ref.at[at(k, c, part, j)], mine.at[k, rows_of(part, j)], load_s.at[n]
        )
        core[k, part, j] = remote(
            d_ref.at[at(k, 1 - c, part, j)], other.at[k, rows_of(part, j)], core_s.at[n], core_r.at[n], peer
        )
        loads[k, part, j].start()

    barrier = pltpu.get_barrier_semaphore()
    for device in (peer, nxt, prv):
        pl.semaphore_signal(barrier, inc=1, device_id={"dp": device}, device_id_type=pl.DeviceIdType.MESH)
    pl.semaphore_wait(barrier, 3)

    urgent = 2 * subs
    for piece in order[:urgent]:
        core[piece].start()

    def pair(k, part, j):
        loads[k, part, j].wait()
        core[k, part, j].wait_recv()
        r = rows_of(part, j)
        mine[k, r, :] = mine[k, r, :] + other[k, r, :]

    def hop(i, k, part, j, device):
        n = i * subs + j
        return remote(mine.at[k, rows_of(part, j)], ring.at[n], ring_s.at[n], ring_r.at[n], device)

    hops = [
        [hop(0, 2, 0, j, nxt) for j in span],
        [hop(1, 2, 1, j, prv) for j in span],
        [hop(2, 1, 1, j, nxt) for j in span],
        [hop(3, 3, 0, j, prv) for j in span],
        [hop(4, 1, 0, j, nxt) for j in span],
        [hop(5, 3, 1, j, prv) for j in span],
    ]
    for j in span:
        pair(2, 0, j)
        hops[0][j].start()
        pair(2, 1, j)
        hops[1][j].start()
    for piece in order[urgent:]:
        core[piece].start()
    for j in span:
        pair(1, 1, j)
        pair(3, 0, j)
    for j in span:
        hops[0][j].wait_send()
        hops[2][j].start()
        hops[1][j].wait_send()
        hops[3][j].start()
    for j in span:
        pair(1, 0, j)
        hops[0][j].wait_recv()
        r = rows_of(0, j)
        mine[1, r, :] = mine[1, r, :] + ring[j]
        hops[4][j].start()
        pair(3, 1, j)
        hops[1][j].wait_recv()
        r = rows_of(1, j)
        mine[3, r, :] = mine[3, r, :] + ring[subs + j]
        hops[5][j].start()
    for j in span:
        pair(0, 0, j)
        pair(0, 1, j)

    def adagrad(part, j, a, b):
        hops[a][j].wait_recv()
        hops[b][j].wait_recv()
        r = rows_of(part, j)
        grad = mine[0, r, :] + (ring[a * subs + j] + ring[b * subs + j])
        new_accum = acc[r, :] + grad * grad
        fresh[r, :] = tab[r, :] - 0.5 * grad / (jnp.sqrt(new_accum) + 1e-08)

    def own_part(i, part, j, device):
        n = i * subs + j
        return remote(fresh.at[rows_of(part, j)], out_ref.at[at(0, c, part, j)], all_s.at[n], all_r.at[n], device)

    def passed(i, k, part, j, device):
        n = i * subs + j
        r = at(k, c, part, j)
        return remote(out_ref.at[r], out_ref.at[r], all_s.at[n], all_r.at[n], device)

    def to_peer(k, part, j):
        n = (k * 2 + part) * subs + j
        r = at(k, c, part, j)
        src = fresh.at[rows_of(part, j)] if k == 0 else out_ref.at[r]
        return remote(src, out_ref.at[r], peer_s.at[n], peer_r.at[n], peer)

    shares = [
        [own_part(0, 0, j, nxt) for j in span],
        [own_part(1, 1, j, nxt) for j in span],
        [own_part(2, 0, j, prv) for j in span],
        [own_part(3, 1, j, prv) for j in span],
        [passed(4, 3, 0, j, nxt) for j in span],
        [passed(5, 1, 1, j, prv) for j in span],
    ]
    peers = [[[to_peer(k, part, j) for j in span] for part in range(2)] for k in range(4)]
    keep = []
    for j in span:
        adagrad(0, j, 3, 4)
        shares[0][j].start()
        adagrad(1, j, 2, 5)
        shares[3][j].start()
        shares[2][j].start()
        shares[1][j].start()
        for part in range(2):
            peers[0][part][j].start()
            keep.append(pltpu.make_async_copy(
                fresh.at[rows_of(part, j)], out_ref.at[at(0, c, part, j)], load_s.at[part * subs + j]))
            keep[-1].start()
    for j in span:
        shares[0][j].wait_recv()
        shares[4][j].start()
        peers[3][0][j].start()
        shares[3][j].wait_recv()
        shares[5][j].start()
        peers[1][1][j].start()
        shares[2][j].wait_recv()
        peers[1][0][j].start()
        shares[1][j].wait_recv()
        peers[3][1][j].start()
    for j in span:
        shares[4][j].wait_recv()
        peers[2][0][j].start()
        shares[5][j].wait_recv()
        peers[2][1][j].start()
    for copy in keep:
        copy.wait()
    for copies in hops[2:] + shares:
        for copy in copies:
            copy.wait_send()
    for k, part, j in order:
        core[k, part, j].wait_send()
        peers[k][part][j].wait()


def update(dense, tab, acc, subs=2):
    rows = dense.shape[0]
    ch = rows // 8
    hbm = pl.BlockSpec(memory_space=pl.ANY)
    vm = pl.BlockSpec(memory_space=pltpu.VMEM)
    dma = pltpu.SemaphoreType.DMA
    return pl.pallas_call(
        functools.partial(update_kernel, subs),
        out_shape=jax.ShapeDtypeStruct((rows, 128), F32),
        in_specs=[hbm, vm, vm],
        out_specs=hbm,
        scratch_shapes=[
            pltpu.VMEM((4, ch, 128), F32),
            pltpu.VMEM((4, ch, 128), F32),
            pltpu.VMEM((6 * subs, ch // 2 // subs, 128), F32),
            pltpu.VMEM((ch, 128), F32),
            dma((8 * subs,)),
            dma((8 * subs,)), dma((8 * subs,)),
            dma((6 * subs,)), dma((6 * subs,)),
            dma((6 * subs,)), dma((6 * subs,)),
            dma((8 * subs,)), dma((8 * subs,)),
        ],
        compiler_params=pltpu.CompilerParams(
            vmem_limit_bytes=UPDATE_VMEM * MIB, collective_id=1, has_side_effects=True
        ),
        name="update",
    )(dense, tab, acc)


def local(queries, positives, neg_ids, table, accum):
    query_grad, received, arrived, tab, acc = exchange(neg_ids, queries, positives, table, accum)
    dense = scatter(received, arrived, table.shape[0])
    return (update(dense, tab, acc), query_grad)


def solution(mesh):
    return jax.shard_map(
        local,
        mesh=mesh,
        in_specs=(
            P(("dp", "own"), None),
            P(("dp", "own"), None),
            P(("dp", "own"), None),
            P("own", None),
            P("own", None),
        ),
        out_specs=(P("own", None), P(("dp", "own"), None)),
        check_vma=False,
    )
```

time: 156 us -> 138 us (0.88)
  Pallas kernels: 145 us -> 132 us
  local copies, waits for them, and re-layouts: 9.93 us -> 5.54 us
    pallas_call x1, Pallas kernels: 87.5 us -> 76.2 us  [exchange(): pl.pallas_call(functools.partial(exchange_kernel, tq), out_shape=(jax.Sha...]
    pallas_call x2 -> x1, Pallas kernels: 50.1 us -> 45.4 us  [update(): pl.pallas_call(functools.partial(update_kernel, subs), out_shape=jax.Shap...]
    unnamed x18 -> x8, local copies, waits for them, and re-layouts: 9.93 us -> 5.54 us
    pallas_call x1, Pallas kernels: 7.42 us -> 10.4 us  [scatter(): pl.pallas_call(scatter_kernel, out_shape=jax.ShapeDtypeStruct((rows_dev,...]
where the time goes in v3:
time: 138 us
  Pallas kernels  132 us (96%)
  local copies, waits for them, and re-layouts  5.54 us (4%)
    pallas_call x1, Pallas kernels, exchange(): pl.pallas_call(functools.partial(exchange_kernel, tq), out_shape=(jax.Sha...  76.2 us
    pallas_call x1, Pallas kernels, update(): pl.pallas_call(functools.partial(update_kernel, subs), out_shape=jax.Shap...  45.4 us
    pallas_call x1, Pallas kernels, scatter(): pl.pallas_call(scatter_kernel, out_shape=jax.ShapeDtypeStruct((rows_dev,...  10.4 us
    unnamed x8, local copies, waits for them, and re-layouts  5.54 us

profile of v3, /device:TPU:1, one launch (start us, length us, event | category | flops | bytes accessed | tf_op | source)
XLA Modules:
  0.0 138.2 jit_solution(10984232975158212919)
XLA Ops:
  0.6 76.2 %exchange.1 = (f32[2048,128]{1,0:T(8,128)}, s32[16,8,128]{2,1,0:T(8,128)}, f32[16,256,128]{2,1,0:T(8,128)}, f32[1024,128]{1,0:T(8,128)}, f32[1024,128]{1,0:T(8,128)}) custom-call(s32[16,512]{1,0:T(8,128)} %raw_ref.1, f32[2048,128]{1,0:T(8,128)} %q_hbm.1, f32[2048,128]{1,0:T(8,128)} %p_hbm.1, f32[8192,128]{1,0:T(8,128)} %table_hbm.1, f32[8192,128]{1,0:T(8,128)} %accum_hbm.1), custom_call_target="tpu_custom_call" | custom-call | tf_op jit(solution)/shard_map/exchange/pallas_call | solution.py:321
  76.8 0.0 copy-start
  76.8 0.0 copy-start.1
  76.9 10.4 %scatter.1.d_ref = f32[8192,128]{1,0:T(8,128)} custom-call(s32[16,8,128]{2,1,0:T(8,128)} %get-tuple-element.7.ids_ref, f32[16,256,128]{2,1,0:T(8,128)} %get-tuple-element.8.grad_hbm), custom_call_target="tpu_custom_call" | custom-call | tf_op jit(solution)/shard_map/scatter/pallas_call | solution.py:100
  87.3 0.0 copy-done
  87.3 0.0 copy-done.1
  87.3 45.4 %update.1 = f32[8192,128]{1,0:T(8,128)} custom-call(f32[8192,128]{1,0:T(8,128)} %scatter.1.d_ref, f32[1024,128]{1,0:T(8,128)S(1)} %copy-done, f32[1024,128]{1,0:T(8,128)S(1)} %copy-done.1), custom_call_target="tpu_custom_call" | custom-call | tf_op jit(solution)/shard_map/update/pallas_call | solution.py:542
  132.7 0.0 copy-start.2
  132.7 4.6 %copy.9 = f32[8192,128]{1,0:T(8,128)} copy(f32[8192,128]{1,0:T(8,128)} %update.1) | data formatting | bytes 8388608
  137.3 0.0 copy-done.2
  137.3 1.0 copy.10
Async XLA Ops:
  76.8 10.5 %copy-start = (f32[1024,128]{1,0:T(8,128)S(1)}, f32[1024,128]{1,0:T(8,128)}, u32[]{:S(2)}) copy-start(f32[1024,128]{1,0:T(8,128)} %get-tuple-element.9.tab) | copy-start | bytes 1572868
  76.8 10.5 %copy-start.1 = (f32[1024,128]{1,0:T(8,128)S(1)}, f32[1024,128]{1,0:T(8,128)}, u32[]{:S(2)}) copy-start(f32[1024,128]{1,0:T(8,128)} %get-tuple-element.10.acc) | copy-start | bytes 1572868
  132.7 4.6 %copy-start.2 = (f32[2048,128]{1,0:T(8,128)S(1)}, f32[2048,128]{1,0:T(8,128)}, u32[]{:S(2)}) copy-start(f32[2048,128]{1,0:T(8,128)} %get-tuple-element.15) | copy-start | bytes 3145732

commit v4 on v3

--- a/solution.py
+++ b/solution.py
@@ -9,7 +9,7 @@
 F32, BF16, I32 = jnp.float32, jnp.bfloat16, jnp.int32
 LOG2E = 1.4426950408889634
 MIB = 1024 * 1024
-UPDATE_VMEM = 52
+UPDATE_VMEM = 48
 SCATTER_VMEM = 55
 
 
@@ -68,32 +68,42 @@
         cnt_ref[r] = jnp.broadcast_to(cnt, (8, few))
 
 
-def scatter_kernel(ids_ref, grad_hbm, out_ref, grad_ref, sems):
+def scatter_kernel(ids_ref, grad_hbm, out_ref, extra_ref, grad_ref, sems):
     owners = grad_hbm.shape[0]
+    gap = owners // 2
 
     def load(s):
         return pltpu.make_async_copy(grad_hbm.at[s], grad_ref.at[s], sems.at[s])
 
     def start(s, c):
         load(s).start()
+        load(s + gap).start()
         return c
 
-    lax.fori_loop(0, owners, start, 0)
+    lax.fori_loop(0, gap, start, 0)
     out_ref[...] = jnp.zeros_like(out_ref)
+    extra_ref[...] = jnp.zeros_like(extra_ref)
 
     def half(s, h):
         for b in range(8):
-            at = [pl.ds(ids_ref[s, h, b * 16 + i], 1) for i in range(16)]
-            vals = [out_ref[at[i], :] + grad_ref[s, pl.ds(h * 128 + b * 16 + i, 1), :] for i in range(16)]
+            at, vals = [], []
+            for total, r in ((out_ref, s), (extra_ref, s + gap)):
+                for i in range(16):
+                    j = b * 16 + i
+                    at.append(pl.ds(ids_ref[r, h, j], 1))
+                    vals.append(total[at[-1], :] + grad_ref[r, pl.ds(h * 128 + j, 1), :])
             for i in range(16):
                 out_ref[at[i], :] = vals[i]
+                extra_ref[at[16 + i], :] = vals[16 + i]
 
     def block(s, c):
         load(s).wait()
+        load(s + gap).wait()
         lax.fori_loop(0, 2, lambda h, c: (half(s, h), c)[1], c)
         return c
 
-    lax.fori_loop(0, owners, block, 0)
+    lax.fori_loop(0, gap, block, 0)
+    out_ref[...] = out_ref[...] + extra_ref[...]
 
 
 def scatter(ids, grads, rows_dev):
@@ -102,7 +112,11 @@
         out_shape=jax.ShapeDtypeStruct((rows_dev, 128), F32),
         in_specs=[pl.BlockSpec(memory_space=pltpu.SMEM), pl.BlockSpec(memory_space=pl.ANY)],
         out_specs=pl.BlockSpec(memory_space=pltpu.VMEM),
-        scratch_shapes=[pltpu.VMEM(grads.shape, F32), pltpu.SemaphoreType.DMA((grads.shape[0],))],
+        scratch_shapes=[
+            pltpu.VMEM((rows_dev, 128), F32),
+            pltpu.VMEM(grads.shape, F32),
+            pltpu.SemaphoreType.DMA((grads.shape[0],)),
+        ],
         compiler_params=pltpu.CompilerParams(vmem_limit_bytes=SCATTER_VMEM * MIB),
         name="scatter",
     )(ids, grads)
@@ -252,8 +266,10 @@
 
     def fetch(s, into):
         def half(h, c):
-            for i in range(128):
-                into[s, pl.ds(h * 128 + i, 1), :] = table_ref[pl.ds(ids_smem[s, h, i], 1), :]
+            for b in range(128 // 32):
+                got = [table_ref[pl.ds(ids_smem[s, h, b * 32 + i], 1), :] for i in range(32)]
+                for i in range(32):
+                    into[s, pl.ds(h * 128 + b * 32 + i, 1), :] = got[i]
             return c
 
         lax.fori_loop(0, 2, half, 0)
@@ -328,7 +344,7 @@
             jax.ShapeDtypeStruct((table.shape[0] // 8, 128), F32),
         ),
         in_specs=[vm, hbm, hbm, hbm, hbm],
-        out_specs=(vm, vm, hbm, hbm, hbm),
+        out_specs=(vm, vm, hbm, vm, vm),
         scratch_shapes=[
             pltpu.VMEM((owners, 8, 128), I32),
             pltpu.VMEM((owners, 8, 256), F32),

time: 138 us -> 135 us (0.978)
  local copies, waits for them, and re-layouts: 5.54 us -> 3 us
    unnamed x8, local copies, waits for them, and re-layouts: 5.54 us -> 3 us
where the time goes in v4:
time: 135 us
  Pallas kernels  131 us (97%)
  local copies, waits for them, and re-layouts  3 us (2%)
    pallas_call x1, Pallas kernels, exchange(): pl.pallas_call(functools.partial(exchange_kernel, tq), out_shape=(jax.Sha...  76.5 us
    pallas_call x1, Pallas kernels, update(): pl.pallas_call(functools.partial(update_kernel, subs), out_shape=jax.Shap...  44.9 us
    pallas_call x1, Pallas kernels, scatter(): pl.pallas_call(scatter_kernel, out_shape=jax.ShapeDtypeStruct((rows_dev,...  9.84 us
    unnamed x8, local copies, waits for them, and re-layouts  3 us

profile of v4, /device:TPU:1, one launch (start us, length us, event | category | flops | bytes accessed | tf_op | source)
XLA Modules:
  0.0 135.0 jit_solution(3763478216552295409)
XLA Ops:
  0.6 76.5 %exchange.1 = (f32[2048,128]{1,0:T(8,128)}, s32[16,8,128]{2,1,0:T(8,128)}, f32[16,256,128]{2,1,0:T(8,128)}, f32[1024,128]{1,0:T(8,128)}, f32[1024,128]{1,0:T(8,128)}) custom-call(s32[16,512]{1,0:T(8,128)} %raw_ref.1, f32[2048,128]{1,0:T(8,128)} %q_hbm.1, f32[2048,128]{1,0:T(8,128)} %p_hbm.1, f32[8192,128]{1,0:T(8,128)} %table_hbm.1, f32[8192,128]{1,0:T(8,128)} %accum_hbm.1), custom_call_target="tpu_custom_call" | custom-call | tf_op jit(solution)/shard_map/exchange/pallas_call | solution.py:337
  77.2 0.0 copy-start
  77.2 0.0 copy-start.1
  77.2 9.8 %scatter.1.d_ref = f32[8192,128]{1,0:T(8,128)} custom-call(s32[16,8,128]{2,1,0:T(8,128)} %get-tuple-element.7.ids_ref, f32[16,256,128]{2,1,0:T(8,128)} %get-tuple-element.8.grad_hbm), custom_call_target="tpu_custom_call" | custom-call | tf_op jit(solution)/shard_map/scatter/pallas_call | solution.py:110
  87.0 0.0 copy-done
  87.1 0.0 copy-done.1
  87.1 44.9 %update.1 = f32[8192,128]{1,0:T(8,128)S(1)} custom-call(f32[8192,128]{1,0:T(8,128)} %scatter.1.d_ref, f32[1024,128]{1,0:T(8,128)S(1)} %copy-done, f32[1024,128]{1,0:T(8,128)S(1)} %copy-done.1), custom_call_target="tpu_custom_call" | custom-call | tf_op jit(solution)/shard_map/update/pallas_call | solution.py:558
  132.0 0.0 copy-start.2
  132.0 2.0 %copy.9 = f32[8192,128]{1,0:T(8,128)} copy(f32[8192,128]{1,0:T(8,128)S(1)} %update.1) | data formatting | bytes 8388608
  134.0 0.0 copy-done.2
  134.0 1.0 copy.10
Async XLA Ops:
  77.2 9.9 %copy-start = (f32[1024,128]{1,0:T(8,128)S(1)}, f32[1024,128]{1,0:T(8,128)}, u32[]{:S(2)}) copy-start(f32[1024,128]{1,0:T(8,128)} %get-tuple-element.9.tab) | copy-start | bytes 1572868
  77.2 9.9 %copy-start.1 = (f32[1024,128]{1,0:T(8,128)S(1)}, f32[1024,128]{1,0:T(8,128)}, u32[]{:S(2)}) copy-start(f32[1024,128]{1,0:T(8,128)} %get-tuple-element.10.acc) | copy-start | bytes 1572868
  132.0 2.0 %copy-start.2 = (f32[2048,128]{1,0:T(8,128)S(1)}, f32[2048,128]{1,0:T(8,128)}, u32[]{:S(2)}) copy-start(f32[2048,128]{1,0:T(8,128)} %get-tuple-element.15) | copy-start | bytes 3145732

commit v5 on v4

--- a/solution.py
+++ b/solution.py
@@ -203,11 +203,13 @@
     x, y = me // 4, me % 4
 
     def up(s):
-        dx, dy = s % 4, (s + s // 4) % 4
+        t = 7 * s % owners
+        dx, dy = t % 4, (t + t // 4) % 4
         return ((x + dx) % 4) * 4 + (y + dy) % 4
 
     def down(s):
-        dx, dy = s % 4, (s + s // 4) % 4
+        t = 7 * s % owners
+        dx, dy = t % 4, (t + t // 4) % 4
         return ((x + 4 - dx) % 4) * 4 + (y + 4 - dy) % 4
 
     def remote(src, dst, send, recv, device):

time: 135 us -> 134 us (level)
  Pallas kernels: 131 us -> 129 us
    pallas_call x1, Pallas kernels: 44.9 us -> 43.4 us  [update(): pl.pallas_call(functools.partial(update_kernel, subs), out_shape=jax.Shap...]
where the time goes in v5:
time: 134 us; the launch traced here: 133 us
  Pallas kernels  129 us (96%)
  local copies, waits for them, and re-layouts  3 us (2%)
    pallas_call x1, Pallas kernels, exchange(): pl.pallas_call(functools.partial(exchange_kernel, tq), out_shape=(jax.Sha...  76 us
    pallas_call x1, Pallas kernels, update(): pl.pallas_call(functools.partial(update_kernel, subs), out_shape=jax.Shap...  43.4 us
    pallas_call x1, Pallas kernels, scatter(): pl.pallas_call(scatter_kernel, out_shape=jax.ShapeDtypeStruct((rows_dev,...  9.83 us
    unnamed x8, local copies, waits for them, and re-layouts  3 us

profile of v5, /device:TPU:1, one launch (start us, length us, event | category | flops | bytes accessed | tf_op | source)
XLA Modules:
  0.0 132.9 jit_solution(12548467544272226392)
XLA Ops:
  0.6 76.0 %exchange.1 = (f32[2048,128]{1,0:T(8,128)}, s32[16,8,128]{2,1,0:T(8,128)}, f32[16,256,128]{2,1,0:T(8,128)}, f32[1024,128]{1,0:T(8,128)}, f32[1024,128]{1,0:T(8,128)}) custom-call(s32[16,512]{1,0:T(8,128)} %raw_ref.1, f32[2048,128]{1,0:T(8,128)} %q_hbm.1, f32[2048,128]{1,0:T(8,128)} %p_hbm.1, f32[8192,128]{1,0:T(8,128)} %table_hbm.1, f32[8192,128]{1,0:T(8,128)} %accum_hbm.1), custom_call_target="tpu_custom_call" | custom-call | tf_op jit(solution)/shard_map/exchange/pallas_call | solution.py:339
  76.6 0.0 copy-start
  76.6 0.0 copy-start.1
  76.6 9.8 %scatter.1.d_ref = f32[8192,128]{1,0:T(8,128)} custom-call(s32[16,8,128]{2,1,0:T(8,128)} %get-tuple-element.7.ids_ref, f32[16,256,128]{2,1,0:T(8,128)} %get-tuple-element.8.grad_hbm), custom_call_target="tpu_custom_call" | custom-call | tf_op jit(solution)/shard_map/scatter/pallas_call | solution.py:110
  86.5 0.0 copy-done
  86.5 0.0 copy-done.1
  86.5 43.4 %update.1 = f32[8192,128]{1,0:T(8,128)S(1)} custom-call(f32[8192,128]{1,0:T(8,128)} %scatter.1.d_ref, f32[1024,128]{1,0:T(8,128)S(1)} %copy-done, f32[1024,128]{1,0:T(8,128)S(1)} %copy-done.1), custom_call_target="tpu_custom_call" | custom-call | tf_op jit(solution)/shard_map/update/pallas_call | solution.py:560
  129.9 0.0 copy-start.2
  129.9 2.0 %copy.9 = f32[8192,128]{1,0:T(8,128)} copy(f32[8192,128]{1,0:T(8,128)S(1)} %update.1) | data formatting | bytes 8388608
  131.9 0.0 copy-done.2
  131.9 1.0 copy.10
Async XLA Ops:
  76.6 9.9 %copy-start = (f32[1024,128]{1,0:T(8,128)S(1)}, f32[1024,128]{1,0:T(8,128)}, u32[]{:S(2)}) copy-start(f32[1024,128]{1,0:T(8,128)} %get-tuple-element.9.tab) | copy-start | bytes 1572868
  76.6 9.9 %copy-start.1 = (f32[1024,128]{1,0:T(8,128)S(1)}, f32[1024,128]{1,0:T(8,128)}, u32[]{:S(2)}) copy-start(f32[1024,128]{1,0:T(8,128)} %get-tuple-element.10.acc) | copy-start | bytes 1572868
  129.9 2.0 %copy-start.2 = (f32[2048,128]{1,0:T(8,128)S(1)}, f32[2048,128]{1,0:T(8,128)}, u32[]{:S(2)}) copy-start(f32[2048,128]{1,0:T(8,128)} %get-tuple-element.15) | copy-start | bytes 3145732

commit v6 on v5

--- a/solution.py
+++ b/solution.py
@@ -68,7 +68,7 @@
         cnt_ref[r] = jnp.broadcast_to(cnt, (8, few))
 
 
-def scatter_kernel(ids_ref, grad_hbm, out_ref, extra_ref, grad_ref, sems):
+def scatter_kernel(ids_ref, grad_hbm, qg_hbm, dense_hbm, qg_out, out_ref, extra_ref, grad_ref, qg_ref, sems, out_s, qg_s):
     owners = grad_hbm.shape[0]
     gap = owners // 2
 
@@ -81,8 +81,13 @@
         return c
 
     lax.fori_loop(0, gap, start, 0)
+    qg_in = pltpu.make_async_copy(qg_hbm, qg_ref, qg_s.at[0])
+    qg_in.start()
     out_ref[...] = jnp.zeros_like(out_ref)
     extra_ref[...] = jnp.zeros_like(extra_ref)
+    qg_in.wait()
+    qg_back = pltpu.make_async_copy(qg_ref, qg_out, qg_s.at[1])
+    qg_back.start()
 
     def half(s, h):
         for b in range(8):
@@ -103,23 +108,40 @@
         return c
 
     lax.fori_loop(0, gap, block, 0)
-    out_ref[...] = out_ref[...] + extra_ref[...]
-
-
-def scatter(ids, grads, rows_dev):
+    size = out_ref.shape[0] // 8
+    parts = []
+    for k in range(8):
+        r = pl.ds(k * size, size)
+        out_ref[r, :] = out_ref[r, :] + extra_ref[r, :]
+        parts.append(pltpu.make_async_copy(out_ref.at[r], dense_hbm.at[r], out_s.at[k]))
+        parts[k].start()
+    for part in parts:
+        part.wait()
+    qg_back.wait()
+
+
+def scatter(ids, grads, query_grad, rows_dev):
+    hbm = pl.BlockSpec(memory_space=pl.ANY)
     return pl.pallas_call(
         scatter_kernel,
-        out_shape=jax.ShapeDtypeStruct((rows_dev, 128), F32),
-        in_specs=[pl.BlockSpec(memory_space=pltpu.SMEM), pl.BlockSpec(memory_space=pl.ANY)],
-        out_specs=pl.BlockSpec(memory_space=pltpu.VMEM),
+        out_shape=(
+            jax.ShapeDtypeStruct((rows_dev, 128), F32),
+            jax.ShapeDtypeStruct(query_grad.shape, F32),
+        ),
+        in_specs=[pl.BlockSpec(memory_space=pltpu.SMEM), hbm, hbm],
+        out_specs=(hbm, hbm),
         scratch_shapes=[
             pltpu.VMEM((rows_dev, 128), F32),
+            pltpu.VMEM((rows_dev, 128), F32),
             pltpu.VMEM(grads.shape, F32),
+            pltpu.VMEM(query_grad.shape, F32),
             pltpu.SemaphoreType.DMA((grads.shape[0],)),
+            pltpu.SemaphoreType.DMA((8,)),
+            pltpu.SemaphoreType.DMA((2,)),
         ],
         compiler_params=pltpu.CompilerParams(vmem_limit_bytes=SCATTER_VMEM * MIB),
         name="scatter",
-    )(ids, grads)
+    )(ids, grads, query_grad)
 
 
 def prepare(q_ref, p_ref, qtf, ptf, qt2, m, total, qacc):
@@ -582,7 +604,7 @@
 
 def local(queries, positives, neg_ids, table, accum):
     query_grad, received, arrived, tab, acc = exchange(neg_ids, queries, positives, table, accum)
-    dense = scatter(received, arrived, table.shape[0])
+    dense, query_grad = scatter(received, arrived, query_grad, table.shape[0])
     return (update(dense, tab, acc), query_grad)
 
 

time: 134 us -> 136 us (1.015)
    unnamed x8 -> x5, local copies, waits for them, and re-layouts: 3 us -> 4.09 us
where the time goes in v6:
time: 136 us; the launch traced here: 134 us
  Pallas kernels  130 us (96%)
  local copies, waits for them, and re-layouts  4.09 us (3%)
    pallas_call x1, Pallas kernels, exchange(): pl.pallas_call(functools.partial(exchange_kernel, tq), out_shape=(jax.Sha...  76 us
    pallas_call x1, Pallas kernels, update(): pl.pallas_call(functools.partial(update_kernel, subs), out_shape=jax.Shap...  43.3 us
    pallas_call x1, Pallas kernels, scatter(): pl.pallas_call(scatter_kernel, out_shape=(jax.ShapeDtypeStruct((rows_dev,...  10.4 us
    unnamed x5, local copies, waits for them, and re-layouts  4.09 us

profile of v6, /device:TPU:1, one launch (start us, length us, event | category | flops | bytes accessed | tf_op | source)
XLA Modules:
  0.0 134.4 jit_solution(15568667482918462255)
XLA Ops:
  0.6 76.0 %exchange.1 = (f32[2048,128]{1,0:T(8,128)}, s32[16,8,128]{2,1,0:T(8,128)}, f32[16,256,128]{2,1,0:T(8,128)}, f32[1024,128]{1,0:T(8,128)}, f32[1024,128]{1,0:T(8,128)}) custom-call(s32[16,512]{1,0:T(8,128)} %raw_ref.1, f32[2048,128]{1,0:T(8,128)} %q_hbm.1, f32[2048,128]{1,0:T(8,128)} %p_hbm.1, f32[8192,128]{1,0:T(8,128)} %table_hbm.1, f32[8192,128]{1,0:T(8,128)} %accum_hbm.1), custom_call_target="tpu_custom_call" | custom-call | tf_op jit(solution)/shard_map/exchange/pallas_call | solution.py:361
  76.6 10.4 %scatter.1 = (f32[8192,128]{1,0:T(8,128)}, f32[2048,128]{1,0:T(8,128)}) custom-call(s32[16,8,128]{2,1,0:T(8,128)} %get-tuple-element.9.ids_ref, f32[16,256,128]{2,1,0:T(8,128)} %get-tuple-element.10.grad_hbm, f32[2048,128]{1,0:T(8,128)} %get-tuple-element.11.qg_hbm), custom_call_target="tpu_custom_call" | custom-call | tf_op jit(solution)/shard_map/scatter/pallas_call | solution.py:125
  87.1 0.0 copy-start
  87.1 1.0 copy-done
  88.1 0.0 copy-start.1
  88.1 1.0 copy-done.1
  89.1 43.3 %update.1 = f32[8192,128]{1,0:T(8,128)S(1)} custom-call(f32[8192,128]{1,0:T(8,128)} %get-tuple-element.12.d_ref, f32[1024,128]{1,0:T(8,128)S(1)} %copy-done, f32[1024,128]{1,0:T(8,128)S(1)} %copy-done.1), custom_call_target="tpu_custom_call" | custom-call | tf_op jit(solution)/shard_map/update/pallas_call | solution.py:582
  132.4 2.0 %copy.8 = f32[8192,128]{1,0:T(8,128)} copy(f32[8192,128]{1,0:T(8,128)S(1)} %update.1) | data formatting | bytes 8388608
Async XLA Ops:
  87.1 1.0 copy-start
  88.1 1.0 copy-start.1
